TPU v7x, 32 devices: a whole 2x2x4 slice. The times are simulated.
32 devices in a mesh: scan: 2 (over y), slab: 4 (over z), coil: 4 (over x, core).
Axes of the slice: x: 2, y: 2, z: 4, core: 2. Of those that a mesh axis runs over, the one named last changes fastest.
Arguments:
- coil_maps: float32 [16, 4, 2, 384, 384], P('coil', 'scan', None, 'slab'), parts along dimension 1, may hold values from -5 to 5
- samples: float32 [16, 4, 1024, 128], P('coil', 'scan', 'slab'), parts along dimension 1, may hold values from -6 to 6
- kernel: float32 [128, 128], replicated, may hold values from -2 to 3
- tile_block: int32 [1024], P('slab'), may hold values from 0 to 575
- tile_count: int32 [1024], P('slab'), may hold values from 32 to 128
- dcf_level: int32 [1024], P('slab'), may hold values from 0 to 15
- dcf_table: float32 [16], replicated, may hold values from 0.2 to 5
Outputs:
- solution: float32 [4, 2, 384, 384], P('scan', None, 'slab'), parts along dimension 0
- residual: float32 [4, 2, 384, 384], P('scan', None, 'slab'), parts along dimension 0
There are 2 independent parts, one for each index of `scan`. A program takes and returns all parts, laid end to end along the dimension named above; an argument that names none is the same for every part. Nothing has to cross between parts.
All inputs are finite; a program needn't handle non-finite values.
Results may differ from a plain program's by a relative error of at most 0.00018.
Values sent between devices are 32-bit elements; how exact they have to be, the bound alone decides.
A program may use at most 128 MiB of HBM per device.

v0:
```python
import math

import jax
import jax.numpy as jnp
from jax import lax
from jax.sharding import PartitionSpec as P

ITERS = 2


HIGH = lax.Precision.HIGHEST
SHIFT = 0.5


def tables(count):
    index = jnp.arange(count, dtype=jnp.int32)
    phase = index[:, None] * index[None, :] % count
    angle = phase.astype(jnp.float32) * (2.0 * math.pi / count)
    factor = 1.0 / math.sqrt(count)
    return (jnp.cos(angle) * factor, jnp.sin(angle) * factor)


def transform(real, imag, cosine, sine, sign, form):
    rc = jnp.einsum(form, real, cosine, precision=HIGH)
    rs = jnp.einsum(form, real, sine, precision=HIGH)
    mc = jnp.einsum(form, imag, cosine, precision=HIGH)
    ms = jnp.einsum(form, imag, sine, precision=HIGH)
    return (rc - sign * ms, mc + sign * rs)


def body(coil_maps, samples, kernel, tile_block, tile_count, dcf_level, dcf_table):
    ncoil, _, xpos, zdev, ylen = coil_maps.shape
    blocklen = kernel.shape[0]
    slabs = lax.axis_size("slab")
    zlen = zdev * slabs
    ky_dev = ylen // slabs
    nblocks = xpos * ky_dev * (zlen // blocklen)
    cos_y, sin_y = tables(ylen)
    cos_z, sin_z = tables(zlen)
    levels = jnp.arange(dcf_table.shape[0], dtype=jnp.int32)
    density = jnp.sum(
        jnp.where(dcf_level[:, None] == levels[None, :], dcf_table[None, :], 0.0), axis=1
    )
    valid = (jnp.arange(blocklen, dtype=jnp.int32)[None, :] < tile_count[:, None]).astype(
        jnp.float32
    )
    weight = density[:, None] * valid
    map_r = coil_maps[:, 0]
    map_i = coil_maps[:, 1]

    def inverse_y(piece):
        out_r, out_i = transform(piece[:, 0], piece[:, 1], cos_y, sin_y, 1.0, "cxzn,nk->cxzk")
        return jnp.stack((out_r, out_i), 1)

    def to_image(values):
        back = jnp.einsum("cita,ab->citb", values, kernel, precision=HIGH)
        blank = jnp.zeros((ncoil, 2, nblocks, blocklen), jnp.float32)
        grid = blank.at[:, :, tile_block].add(back).reshape(ncoil, 2, xpos, ky_dev, zlen)
        part_r, part_i = transform(grid[:, 0], grid[:, 1], cos_z, sin_z, 1.0, "cxyk,zk->cxzy")
        spectra = jnp.stack((part_r, part_i), 1)
        coils = inverse_y(lax.all_to_all(spectra, "slab", split_axis=3, concat_axis=4, tiled=True))
        coil_r = coils[:, 0]
        coil_i = coils[:, 1]
        sum_r = jnp.sum(map_r * coil_r + map_i * coil_i, axis=0)
        sum_i = jnp.sum(map_r * coil_i - map_i * coil_r, axis=0)
        return jnp.stack((sum_r, sum_i), 0)

    rhs_local = to_image(samples * weight)

    def total(local):
        return lax.psum(local, "coil")

    def inner(first, second):
        return lax.psum(jnp.sum(first * second), "slab")

    rhs = total(rhs_local)
    solution = jnp.zeros_like(rhs)
    residual = rhs
    direction = rhs
    norm_now = inner(residual, residual)
    for step in range(ITERS):
        sample_coil_r = map_r * direction[0][None] - map_i * direction[1][None]
        sample_coil_i = map_r * direction[1][None] + map_i * direction[0][None]
        spec_r, spec_i = transform(
            sample_coil_r, sample_coil_i, cos_y, sin_y, -1.0, "cxzn,nk->cxzk"
        )
        sample_spectra = jnp.stack((spec_r, spec_i), 1)
        forward_piece = lax.all_to_all(
            sample_spectra, "slab", split_axis=4, concat_axis=3, tiled=True
        )
        forward_out_r, forward_out_i = transform(
            forward_piece[:, 0], forward_piece[:, 1], cos_z, sin_z, -1.0, "cxzy,zk->cxyk"
        )
        sample_grid = jnp.stack((forward_out_r, forward_out_i), 1)
        blocks = sample_grid.reshape(ncoil, 2, nblocks, blocklen)
        picked = blocks[:, :, tile_block]
        image = (
            total(to_image(jnp.einsum("citb,ab->cita", picked, kernel, precision=HIGH) * weight))
            + SHIFT * direction
        )
        alpha = norm_now / inner(direction, image)
        solution = solution + alpha * direction
        residual = residual - alpha * image
        norm_next = inner(residual, residual)
        direction = residual + norm_next / norm_now * direction
        norm_now = norm_next
    return (solution, residual)


def solution(mesh):
    placed = (
        P("coil", "scan", None, "slab", None),
        P("coil", "scan", "slab", None),
        P(),
        P("slab"),
        P("slab"),
        P("slab"),
        P(),
    )
    return jax.shard_map(
        body,
        mesh=mesh,
        in_specs=placed,
        out_specs=(P("scan", None, "slab", None), P("scan", None, "slab", None)),
        check_vma=False,
    )
```

profile of v0, /device:TPU:0, one launch (start us, length us, event | category | flops | bytes accessed | tf_op | source)
XLA Modules:
  0.0 874.4 jit_solution(3785266412244175420)
XLA Ops:
  13.4 12.0 %scatter_fusion = f32[4,2,576,128]{3,0,2,1:T(4,128)S(1)} fusion(f32[4,2,576,128]{3,0,2,1:T(4,128)S(1)} %broadcast.52.clone, s32[256]{0:T(256)S(1)} %compare_select_fusion, f32[256,4,2,128]{3,1,2,0:T(4,128)S(1)} %copy.64), kind=kCustom, calls=%fused_computation.2 | custom fusion | flops 262144 | bytes 3146752 | tf_op jit(solution)/shard_map/scatter-add | solution.py:58
  38.7 5.1 fusion.12
  43.8 4.6 fusion.13
  54.5 76.8 %all_to_all.90 = f32[4,2,2,384,96]{4,2,0,1,3:T(2,128)S(1)} all-to-all(f32[4,2,2,384,96]{4,2,0,1,3:T(2,128)S(1)} %copy.66), channel_id=1, replica_groups=mesh['scan'=2,'slab'=4,'coil'=4] {'slab'}, dimensions={3} | all-to-all | bytes 4718592 | tf_op jit(solution)/shard_map/all_to_all | solution.py:61
  136.1 6.0 fusion.36
  142.1 4.7 fusion.37
  146.8 4.9 convolution_subtract_fusion.4
  151.7 4.9 fusion.19
  157.6 32.9 %all-reduce.5.cloned.1.call-done = f32[2,2,96,384]{3,2,1,0:T(8,128)} async-done(((f32[2,2,96,384]{3,2,1,0:T(8,128)}), f32[2,2,96,384]{3,2,1,0:T(8,128)}) %all-reduce.5.cloned.1.call-update) | async-done | bytes 589840 | tf_op jit(solution)/shard_map/psum | solution.py:71
  191.6 5.2 fusion.93
  196.8 4.8 fusion.91
  201.6 4.8 fusion.11
  206.4 5.5 fusion.9
  215.5 4.6 all-to-all-start.1
  220.1 69.7 %all-to-all-done.1 = f32[4,2,2,96,384]{3,2,0,1,4:T(2,128)S(1)} async-done(((f32[4,2,2,96,384]{3,2,0,1,4:T(2,128)}), f32[4,2,2,96,384]{3,2,0,1,4:T(2,128)S(1)}, u32[]{:S(2)}, u32[]{:S(2)}) %all-to-all-start.1) | async-done | bytes 2359328 | tf_op jit(solution)/shard_map/all_to_all | solution.py:88
  296.9 4.6 fusion.38
  301.4 5.6 fusion.39
  307.0 6.0 fusion.7
  318.6 5.6 fusion.6
  332.6 12.0 %scatter_fusion.1 = f32[4,2,576,128]{3,0,2,1:T(4,128)S(1)} fusion(f32[4,2,576,128]{3,0,2,1:T(4,128)S(1)} %broadcast.52.clone.1, s32[256]{0:T(256)S(1)} %compare_select_fusion, f32[256,4,2,128]{3,1,2,0:T(4,128)S(1)} %copy.74), kind=kCustom, calls=%fused_computation.3 | custom fusion | flops 262144 | bytes 3146752 | tf_op jit(solution)/shard_map/scatter-add | solution.py:58
  357.8 4.8 fusion.14
  362.6 4.6 fusion.15
  373.2 72.7 %all_to_all.91 = f32[4,2,2,384,96]{4,2,0,1,3:T(2,128)S(1)} all-to-all(f32[4,2,2,384,96]{4,2,0,1,3:T(2,128)S(1)} %copy.76), channel_id=1, replica_groups=mesh['scan'=2,'slab'=4,'coil'=4] {'slab'}, dimensions={3} | all-to-all | bytes 4718592 | tf_op jit(solution)/shard_map/all_to_all | solution.py:61
  451.0 6.0 fusion.42
  457.0 4.7 fusion.43
  461.7 4.9 convolution_subtract_fusion.2
  466.6 5.0 fusion.25
  472.6 31.6 %all-reduce.7.cloned.1.call-done = f32[2,2,96,384]{3,2,1,0:T(8,128)} async-done(((f32[2,2,96,384]{3,2,1,0:T(8,128)}), f32[2,2,96,384]{3,2,1,0:T(8,128)}) %all-reduce.7.cloned.1.call-update) | async-done | bytes 589840 | tf_op jit(solution)/shard_map/psum | solution.py:71
  506.1 12.3 %all-reduce = (f32[]{:T(128)}, f32[]{:T(128)}) all-reduce(f32[]{:T(128)} %get-tuple-element.9, f32[]{:T(128)} %get-tuple-element.8), channel_id=1, replica_groups=mesh['scan'=2,'slab'=4,'coil'=4] {'slab'}, use_global_device_ids=true, to_apply=%region_6.7 | all-reduce | flops 2 | bytes 16 | tf_op jit(solution)/shard_map/psum | solution.py:74
  520.5 9.0 %psum.53 = f32[]{:T(128)} all-reduce(f32[]{:T(128)} %multiply_reduce_fusion.1), channel_id=1, replica_groups=mesh['scan'=2,'slab'=4,'coil'=4] {'slab'}, use_global_device_ids=true, to_apply=%region_14.15 | all-reduce | flops 1 | bytes 8 | tf_op jit(solution)/shard_map/psum | solution.py:74
  532.8 4.7 fusion.83
  537.5 4.7 fusion.81
  542.3 5.2 fusion.5
  547.5 4.8 fusion.3
  555.9 69.9 %all_to_all.92 = f32[4,2,2,96,384]{3,2,0,1,4:T(2,128)S(1)} all-to-all(f32[4,2,2,96,384]{3,2,0,1,4:T(2,128)} %copy.78), channel_id=1, replica_groups=mesh['scan'=2,'slab'=4,'coil'=4] {'slab'}, dimensions={4} | all-to-all | bytes 4718592 | tf_op jit(solution)/shard_map/all_to_all | solution.py:88
  637.6 5.6 fusion.45
  643.2 6.0 fusion.1
  654.7 5.6 fusion
  670.9 22.4 %scatter_fusion.2 = f32[4,2,576,128]{3,0,2,1:T(4,128)S(1)} fusion(f32[4,2,576,128]{3,0,2,1:T(4,128)S(1)} %broadcast.52, s32[256]{0:T(256)S(1)} %compare_select_fusion, f32[256,4,2,128]{3,1,2,0:T(4,128)} %copy.83), kind=kCustom, calls=%fused_computation.4 | custom fusion | flops 262144 | bytes 3146752 | tf_op jit(solution)/shard_map/scatter-add | solution.py:58
  706.5 4.8 fusion.16
  711.3 4.6 fusion.17
  719.6 72.0 %all_to_all.93 = f32[4,2,2,384,96]{4,2,0,1,3:T(2,128)S(1)} all-to-all(f32[4,2,2,384,96]{4,2,0,1,3:T(2,128)} %copy.85), channel_id=1, replica_groups=mesh['scan'=2,'slab'=4,'coil'=4] {'slab'}, dimensions={3} | all-to-all | bytes 4718592 | tf_op jit(solution)/shard_map/all_to_all | solution.py:61
  799.0 4.6 fusion.48
  803.6 4.7 fusion.49
  808.3 4.9 convolution_subtract_fusion
  813.2 5.0 fusion.31
  819.1 31.8 %all-reduce.9.cloned.1.call-done = f32[2,2,96,384]{3,2,1,0:T(8,128)} async-done(((f32[2,2,96,384]{3,2,1,0:T(8,128)}), f32[2,2,96,384]{3,2,1,0:T(8,128)}) %all-reduce.9.cloned.1.call-update) | async-done | bytes 589840 | tf_op jit(solution)/shard_map/psum | solution.py:71
  852.8 12.3 %psum.55 = f32[]{:T(128)} all-reduce(f32[]{:T(128)} %multiply_reduce_fusion), channel_id=1, replica_groups=mesh['scan'=2,'slab'=4,'coil'=4] {'slab'}, use_global_device_ids=true, to_apply=%region_20.21 | all-reduce | flops 1 | bytes 8 | tf_op jit(solution)/shard_map/psum | solution.py:74
  (114 shorter events, 146.2 us)
Async XLA Ops:
  7.2 3.0 copy-start
  7.2 183.3 %all-reduce.5.cloned.1.call-start = ((), (), s32[]{:S(2)}) async-start(), calls=%async_computation.5 | async-start | bytes 1179648 | tf_op jit(solution)/shard_map/psum | solution.py:71
  9.5 0.7 copy-start.15
  136.1 6.0 copy-start.10
  146.8 5.0 copy-start.6
  215.5 74.3 %all-to-all-start.1 = ((f32[4,2,2,96,384]{3,2,0,1,4:T(2,128)}), f32[4,2,2,96,384]{3,2,0,1,4:T(2,128)S(1)}, u32[]{:S(2)}, u32[]{:S(2)}) async-start(f32[4,2,2,96,384]{3,2,0,1,4:T(2,128)} %copy.69), calls=%async_computation.1 | async-start | bytes 6291456 | tf_op jit(solution)/shard_map/all_to_all | solution.py:88
  220.1 284.1 %all-reduce.7.cloned.1.call-start = ((), (), s32[]{:S(2)}) async-start(), calls=%async_computation.6 | async-start | bytes 1179648 | tf_op jit(solution)/shard_map/psum | solution.py:71
  315.4 3.2 copy-start.17
  325.5 1.3 copy-start.12
  451.0 6.0 copy-start.11
  461.7 4.9 copy-start.7
  471.6 32.6 %copy-start.1 = (f32[2,2,96,384]{3,2,1,0:T(8,128)S(1)}, f32[2,2,96,384]{3,2,1,0:T(8,128)}, u32[]{:S(2)}) copy-start(f32[2,2,96,384]{3,2,1,0:T(8,128)} %all-reduce.5.cloned.1.call-done) | copy-start | bytes 1769476
  472.5 378.3 %all-reduce.9.cloned.1.call-start = ((), (), s32[]{:S(2)}) async-start(), calls=%async_computation.7 | async-start | bytes 1179648 | tf_op jit(solution)/shard_map/psum | solution.py:71
  504.2 15.5 %copy-start.2 = (f32[2,2,96,384]{3,2,1,0:T(8,128)S(1)}, f32[2,2,96,384]{3,2,1,0:T(8,128)}, u32[]{:S(2)}) copy-start(f32[2,2,96,384]{3,2,1,0:T(8,128)} %all-reduce.7.cloned.1.call-done) | copy-start | bytes 1769476
  530.9 1.9 copy-start.8
  531.0 0.8 copy-start.4
  651.5 3.2 copy-start.18
  661.7 1.3 copy-start.13
  663.5 2.3 copy-start.16
  808.3 4.9 copy-start.9
  818.2 32.7 %copy-start.5 = (f32[2,2,96,384]{3,2,1,0:T(8,128)S(1)}, f32[2,2,96,384]{3,2,1,0:T(8,128)}, u32[]{:S(2)}) copy-start(f32[2,2,96,384]{3,2,1,0:T(8,128)} %copy-done.4) | copy-start | bytes 1769476
  819.1 47.3 %copy-start.3 = (f32[2,2,96,384]{3,2,1,0:T(8,128)S(1)}, f32[2,2,96,384]{3,2,1,0:T(8,128)}, u32[]{:S(2)}) copy-start(f32[2,2,96,384]{3,2,1,0:T(8,128)} %all-reduce.7.cloned.1.call-done) | copy-start | bytes 1769476
  850.9 15.5 %copy-start.14 = (f32[2,2,96,384]{3,2,1,0:T(8,128)S(1)}, f32[2,2,96,384]{3,2,1,0:T(8,128)}, u32[]{:S(2)}) copy-start(f32[2,2,96,384]{3,2,1,0:T(8,128)} %all-reduce.9.cloned.1.call-done) | copy-start | bytes 1769476
Sparse Core Ops, SparseCore 0:
  157.7 32.7 all-reduce.4
  472.7 31.5 all-reduce.6
  819.2 31.6 all-reduce.8
where the time goes:
time: 880 us; the launch traced here: 874 us
  blocking collectives  325 us (37%)
  matrix products  207 us (24%)
  waiting for transfers between devices  166 us (19%)
  local copies, waits for them, and re-layouts  91.1 us (10%)
  other arithmetic  61.8 us (7%)
  between operations  18.6 us (2%)
    all_to_all x3, blocking collectives, to_image(): lax.all_to_all(spectra, 'slab', split_axis=3, concat_axis=4, tiled=True)  221 us
    psum x3, waiting for transfers between devices, total(): return lax.psum(local, 'coil')  96.3 us
    all_to_all x1, blocking collectives, body(): lax.all_to_all(sample_spectra, 'slab', split_axis=4, concat_axis=3, tiled...  69.9 us
    all_to_all x1, waiting for transfers between devices, body(): lax.all_to_all(sample_spectra, 'slab', split_axis=4, concat_axis=3, tiled...  69.7 us
    dot_general x10, matrix products, transform(): ms = jnp.einsum(form, imag, sine, precision=HIGH)  51.6 us
    dot_general x10, matrix products, transform(): rs = jnp.einsum(form, real, sine, precision=HIGH)  50.2 us
    dot_general x10, matrix products, transform(): rc = jnp.einsum(form, real, cosine, precision=HIGH)  49 us
    dot_general x10, matrix products, transform(): mc = jnp.einsum(form, imag, cosine, precision=HIGH)  48 us
  transfers between devices with their start and end apart: 4, of which 4 were waited for; matrix products, arithmetic and copies ran while one was open for 0% of the time, Pallas kernels for 0%

commit v1 on v0

--- a/solution.py
+++ b/solution.py
@@ -2,7 +2,11 @@
 
 import jax
 import jax.numpy as jnp
+import ml_dtypes
+import numpy as np
 from jax import lax
+from jax.experimental import pallas as pl
+from jax.experimental.pallas import tpu as pltpu
 from jax.sharding import PartitionSpec as P
 
 ITERS = 2
@@ -107,6 +111,284 @@
     return (solution, residual)
 
 
+RADIX = 3
+F32 = jnp.float32
+BF16 = jnp.bfloat16
+ROOT = math.sqrt(3.0) / 2.0
+
+
+def split(value):
+    high = value.astype(BF16)
+    return high, (value - high.astype(F32)).astype(BF16)
+
+
+def dot(left, right, form=((1,), (0,))):
+    return lax.dot_general(left, right, (form, ((), ())), preferred_element_type=F32)
+
+
+def dot_left(table_high, table_low, value, form=((1,), (0,))):
+    high, low = split(value)
+    return dot(table_high, high, form) + (dot(table_high, low, form) + dot(table_low, high, form))
+
+
+def dot_right(value, table_high, table_low):
+    high, low = split(value)
+    return dot(high, table_high) + (dot(low, table_high) + dot(high, table_low))
+
+
+def butterfly(parts, sign):
+    (a_r, a_i), (b_r, b_i), (c_r, c_i) = parts
+    sum_r, sum_i = b_r + c_r, b_i + c_i
+    dif_r, dif_i = (sign * ROOT) * (b_r - c_r), (sign * ROOT) * (b_i - c_i)
+    mid_r, mid_i = a_r - 0.5 * sum_r, a_i - 0.5 * sum_i
+    return (
+        (a_r + sum_r, a_i + sum_i),
+        (mid_r - dif_i, mid_i + dif_r),
+        (mid_r + dif_i, mid_i - dif_r),
+    )
+
+
+def dft_tables(length):
+    base = length // RADIX
+    index = np.arange(base)
+    whole = np.arange(length)
+    angle = (index[:, None] * whole[None, :] % length) * (2.0 * np.pi / length)
+    real = np.cos(angle) / np.sqrt(length)
+    imag = -np.sin(angle) / np.sqrt(length)
+    tables = []
+    for part in range(RADIX):
+        re, im = real[:, part::RADIX], imag[:, part::RADIX]
+        right = np.block([[re, im], [-im, re]])
+        left = np.block([[re, -im], [im, re]])
+        tables.append((left, left.T, right, right.T))
+    full = np.array(tables, dtype=np.float32)
+    high = full.astype(ml_dtypes.bfloat16)
+    low = (full - high.astype(np.float32)).astype(ml_dtypes.bfloat16)
+    return np.stack((high, low), 2)
+
+
+def mark_blocks(column_ref, marks):
+    step = 256
+    tiles = column_ref.shape[1]
+
+    def fill(chunk, carry):
+        start = pl.multiple_of(chunk * step, step)
+        rows = lax.broadcasted_iota(jnp.int32, (step, tiles), 0) + start
+        marks[pl.ds(start, step), :] = (rows == column_ref[...]).astype(F32).astype(BF16)
+        return carry
+
+    lax.fori_loop(0, marks.shape[0] // step, fill, 0)
+
+
+def add_blocks(back_high, back_low, marks, grid):
+    step = 768
+
+    def chunk(index, carry):
+        start = pl.multiple_of(index * step, step)
+        mark = marks[pl.ds(start, step), :]
+        rows = ((1,), (1,))
+        grid[:, pl.ds(start, step)] = dot(back_high[...], mark, rows) + dot(back_low[...], mark, rows)
+        return carry
+
+    lax.fori_loop(0, marks.shape[0] // step, chunk, 0)
+
+
+def grid_to_image(grid, tables, middle, maps, out):
+    xpos, _, base, length = maps.shape[1:]
+    span = xpos * length
+    for x in range(xpos):
+        lanes = slice(x * length, (x + 1) * length)
+        parts = []
+        for q in range(RADIX):
+            part = grid[:, q * span + x * length : q * span + (x + 1) * length]
+            parts.append((part[:base], part[base:]))
+        for b, (re, im) in enumerate(butterfly(parts, 1.0)):
+            value = jnp.concatenate((re, im), 0)
+            middle[b, :, lanes] = dot_left(tables[b, 1, 0], tables[b, 1, 1], value)
+
+    def rows(index, carry):
+        x, b = index // RADIX, index % RADIX
+        parts = []
+        for r in range(RADIX):
+            start = pl.multiple_of(x * length + r * base, base)
+            value = middle[b, :, pl.ds(start, base)]
+            value = jnp.concatenate((value[:base], value[base:]), 1)
+            back = dot_right(value, tables[r, 3, 0], tables[r, 3, 1])
+            parts.append((back[:, :base], back[:, base:]))
+        for q, (re, im) in enumerate(butterfly(parts, 1.0)):
+            lanes = slice(q * base, (q + 1) * base)
+            map_r, map_i = maps[0, x, b, :, lanes], maps[1, x, b, :, lanes]
+            out[0, x, b, :, lanes] = map_r * re + map_i * im
+            out[1, x, b, :, lanes] = map_r * im - map_i * re
+        return carry
+
+    lax.fori_loop(0, xpos * RADIX, rows, 0)
+
+
+def image_to_grid(image, tables, middle, maps, grid_high, grid_low):
+    xpos, _, base, length = maps.shape[1:]
+    span = xpos * length
+
+    def rows(index, carry):
+        x, b = index // RADIX, index % RADIX
+        parts = []
+        for q in range(RADIX):
+            lanes = slice(q * base, (q + 1) * base)
+            map_r, map_i = maps[0, x, b, :, lanes], maps[1, x, b, :, lanes]
+            re, im = image[0, x, b, :, lanes], image[1, x, b, :, lanes]
+            parts.append((map_r * re - map_i * im, map_r * im + map_i * re))
+        for r, (re, im) in enumerate(butterfly(parts, -1.0)):
+            value = dot_right(jnp.concatenate((re, im), 1), tables[r, 2, 0], tables[r, 2, 1])
+            start = pl.multiple_of(x * length + r * base, base)
+            middle[b, :base, pl.ds(start, base)] = value[:, :base]
+            middle[b, base:, pl.ds(start, base)] = value[:, base:]
+        return carry
+
+    lax.fori_loop(0, xpos * RADIX, rows, 0)
+    for x in range(xpos):
+        parts = []
+        for b in range(RADIX):
+            value = middle[b, :, x * length : (x + 1) * length]
+            value = dot_left(tables[b, 0, 0], tables[b, 0, 1], value)
+            parts.append((value[:base], value[base:]))
+        for q, (re, im) in enumerate(butterfly(parts, -1.0)):
+            high, low = split(jnp.concatenate((re, im), 0))
+            lanes = slice(q * span + x * length, q * span + (x + 1) * length)
+            grid_high[:, lanes] = high
+            grid_low[:, lanes] = low
+
+
+def rhs_kernel(samples, weight, kernel, column, tables, maps, out, marks, back_high, back_low, middle, grid):
+    base = kernel.shape[0]
+    mark_blocks(column, marks)
+    kernel_t = kernel[...].T
+    kernel_high, kernel_low = split(kernel_t)
+    for part in range(2):
+        value = samples[part] * weight[...]
+        back = dot_left(kernel_high, kernel_low, value, ((1,), (1,)))
+        high, low = split(back)
+        back_high[part * base : (part + 1) * base, :] = high
+        back_low[part * base : (part + 1) * base, :] = low
+    add_blocks(back_high, back_low, marks, grid)
+    grid_to_image(grid, tables, middle, maps, out)
+
+
+def normal_kernel(image, weight, kernel, column, tables, maps, out, marks, back_high, back_low, middle, grid, grid_high, grid_low):
+    base = kernel.shape[0]
+    mark_blocks(column, marks)
+    image_to_grid(image, tables, middle, maps, grid_high, grid_low)
+    kernel_high, kernel_low = split(kernel[...])
+    turned_high, turned_low = split(kernel[...].T)
+    step = 256
+
+    def sample(index, carry):
+        start = pl.multiple_of(index * step, step)
+        mark = marks[:, pl.ds(start, step)]
+        picked = dot(grid_high[...], mark) + dot(grid_low[...], mark)
+        for part in range(2):
+            rows = slice(part * base, (part + 1) * base)
+            value = dot_left(kernel_high, kernel_low, picked[rows]) * weight[:, pl.ds(start, step)]
+            high, low = split(dot_left(turned_high, turned_low, value))
+            back_high[rows, pl.ds(start, step)] = high
+            back_low[rows, pl.ds(start, step)] = low
+        return carry
+
+    lax.fori_loop(0, marks.shape[1] // step, sample, 0)
+    add_blocks(back_high, back_low, marks, grid)
+    grid_to_image(grid, tables, middle, maps, out)
+
+
+def call(kernel, image_shape, tiles, forward):
+    base, length = image_shape[-2:]
+    cells = image_shape[1] * RADIX * length
+    scratch = [
+        pltpu.VMEM((cells, tiles), BF16),
+        pltpu.VMEM((2 * base, tiles), BF16),
+        pltpu.VMEM((2 * base, tiles), BF16),
+        pltpu.VMEM((RADIX, 2 * base, image_shape[1] * length), F32),
+        pltpu.VMEM((2 * base, cells), F32),
+    ]
+    if forward:
+        scratch += [pltpu.VMEM((2 * base, cells), BF16)] * 2
+    return pl.pallas_call(
+        kernel,
+        out_shape=jax.ShapeDtypeStruct(image_shape, F32),
+        in_specs=[pl.BlockSpec(memory_space=pltpu.VMEM)] * 6,
+        out_specs=pl.BlockSpec(memory_space=pltpu.VMEM),
+        scratch_shapes=scratch,
+        compiler_params=pltpu.CompilerParams(vmem_limit_bytes=56 * 2**20),
+    )
+
+
+def whole_coils(coil_maps, samples, kernel, tile_block, tile_count, dcf_level, dcf_table):
+    ncoil, _, xpos, zdev, ylen = coil_maps.shape
+    base = kernel.shape[0]
+    slabs = lax.axis_size("slab")
+    slab = lax.axis_index("slab")
+    ky_dev = ylen // slabs
+    lines = zdev // RADIX
+    zblocks = zdev * slabs // base
+
+    near = coil_maps.reshape(ncoil, 2, xpos, lines, RADIX, ylen).transpose(0, 1, 2, 4, 3, 5)
+    maps = lax.all_to_all(near, "slab", split_axis=0, concat_axis=4, tiled=True)[0]
+    data = lax.all_to_all(samples, "slab", split_axis=0, concat_axis=2, tiled=True)[0]
+
+    cells = jnp.stack((tile_block, tile_count, dcf_level))
+    cells = lax.all_gather(cells, "slab", axis=1, tiled=True)
+    block, count, level = cells[0], cells[1], cells[2]
+    tiles = block.shape[0]
+    shard = jnp.arange(tiles, dtype=jnp.int32) // (tiles // slabs)
+    ky = shard * ky_dev + block // zblocks % ky_dev
+    column = (block % zblocks * xpos + block // (zblocks * ky_dev)) * ylen
+    column = (column + ky % RADIX * base + ky // RADIX)[None, :]
+    levels = jnp.arange(dcf_table.shape[0], dtype=jnp.int32)
+    density = jnp.sum(jnp.where(level[:, None] == levels[None, :], dcf_table[None, :], 0.0), axis=1)
+    position = jnp.arange(base, dtype=jnp.int32)
+    weight = jnp.where(position[None, :] < count[:, None], density[:, None], 0.0)
+    weight_t = jnp.where(position[:, None] < count[None, :], density[None, :], 0.0)
+
+    tables = jnp.asarray(dft_tables(ylen))
+    shape = maps.shape
+
+    def total(local):
+        return lax.psum(local, ("slab", "coil"))
+
+    rhs = total(call(rhs_kernel, shape, tiles, False)(data, weight, kernel, column, tables, maps))
+    solution = jnp.zeros_like(rhs)
+    residual = rhs
+    direction = rhs
+    norm_now = jnp.sum(residual * residual)
+    normal = call(normal_kernel, shape, tiles, True)
+    for step in range(ITERS):
+        image = total(normal(direction, weight_t, kernel, column, tables, maps)) + SHIFT * direction
+        alpha = norm_now / jnp.sum(direction * image)
+        solution = solution + alpha * direction
+        residual = residual - alpha * image
+        norm_next = jnp.sum(residual * residual)
+        direction = residual + norm_next / norm_now * direction
+        norm_now = norm_next
+
+    def own(value):
+        piece = lax.dynamic_slice_in_dim(value, slab * lines, lines, 3)
+        return piece.transpose(0, 1, 3, 2, 4).reshape(2, xpos, zdev, ylen)
+
+    return own(solution), own(residual)
+
+
+def fits(mesh, coil_maps, samples, kernel):
+    slabs, coils = mesh.shape["slab"], mesh.shape["coil"]
+    coil_dev = coil_maps.shape[0] // coils
+    zlen, ylen = coil_maps.shape[3:]
+    base = kernel.shape[0]
+    return (
+        coil_dev == slabs
+        and zlen == ylen == RADIX * base
+        and base == 128
+        and zlen % (slabs * RADIX) == 0
+        and samples.shape[2] % 256 == 0
+    )
+
+
 def solution(mesh):
     placed = (
         P("coil", "scan", None, "slab", None),
@@ -117,10 +399,15 @@
         P("slab"),
         P(),
     )
-    return jax.shard_map(
-        body,
-        mesh=mesh,
-        in_specs=placed,
-        out_specs=(P("scan", None, "slab", None), P("scan", None, "slab", None)),
-        check_vma=False,
-    )
+
+    def run(coil_maps, samples, kernel, *rest):
+        chosen = whole_coils if fits(mesh, coil_maps, samples, kernel) else body
+        return jax.shard_map(
+            chosen,
+            mesh=mesh,
+            in_specs=placed,
+            out_specs=(P("scan", None, "slab", None), P("scan", None, "slab", None)),
+            check_vma=False,
+        )(coil_maps, samples, kernel, *rest)
+
+    return run

time: 880 us -> 494 us (0.56)
  blocking collectives: 325 us -> 58.6 us
  matrix products: 207 us -> 0 us
  waiting for transfers between devices: 166 us -> 316 us
  local copies, waits for them, and re-layouts: 91.1 us -> 10.3 us
  Pallas kernels: 0 us -> 60.5 us
  other arithmetic: 61.8 us -> 19.9 us
    all_to_all x4 -> x0, blocking collectives: 291 us -> none  [the longest x3 221 us: to_image(): lax.all_to_all(spectra, 'slab', split_axis=3, concat_axis=4, tiled=True)]
    dot_general x45 -> x0, matrix products: 207 us -> none  [the longest x10 51.6 us: transform(): ms = jnp.einsum(form, imag, sine, precision=HIGH)]
    psum x3, waiting for transfers between devices: 96.3 us -> 295 us  [total(): return lax.psum(local, ('slab', 'coil'))]
    pallas_call x0 -> x3, Pallas kernels: none -> 60.5 us  [the longest x2 47.4 us: whole_coils(): normal(direction, weight_t, kernel, column, tables, maps)]
    all_gather x0 -> x1, blocking collectives: none -> 58.6 us  [whole_coils(): cells = lax.all_gather(cells, 'slab', axis=1, tiled=True)]
    all_to_all x1 -> x2, waiting for transfers between devices: 69.7 us -> 20.8 us  [the longest x1 20.8 us: whole_coils(): lax.all_to_all(samples, 'slab', split_axis=0, concat_axis=2, tiled=True)[0]]
    scatter-add x3 -> x0, other arithmetic: 46.4 us -> none  [to_image(): blank.at[:, :, tile_block].add(back).reshape(ncoil, 2, xpos, ky_dev, zlen)]
    another operation x16 -> x0, local copies, waits for them, and re-layouts: 35.4 us -> none  [the longest x8 15.2 us: body(): sample_grid = jnp.stack((forward_out_r, forward_out_i), 1)]
  transfers between devices with their start and end apart: 4 -> 5, of which waited for: 4 -> 4; matrix products, arithmetic and copies ran while one was open for 0% -> 2% of each run, Pallas kernels for 0% -> 0%
where the time goes in v1:
time: 494 us; the launch traced here: 493 us
  waiting for transfers between devices  316 us (64%)
  Pallas kernels  60.5 us (12%)
  blocking collectives  58.6 us (12%)
  other arithmetic  19.9 us (4%)
  between operations  17.7 us (4%)
  starting transfers between devices  10.6 us (2%)
  local copies, waits for them, and re-layouts  10.3 us (2%)
    psum x3, waiting for transfers between devices, total(): return lax.psum(local, ('slab', 'coil'))  295 us
    all_gather x1, blocking collectives, whole_coils(): cells = lax.all_gather(cells, 'slab', axis=1, tiled=True)  58.6 us
    pallas_call x2, Pallas kernels, whole_coils(): normal(direction, weight_t, kernel, column, tables, maps)  47.4 us
    all_to_all x1, waiting for transfers between devices, whole_coils(): lax.all_to_all(samples, 'slab', split_axis=0, concat_axis=2, tiled=True)[0]  20.8 us
    pallas_call x1, Pallas kernels, whole_coils(): call(rhs_kernel, shape, tiles, False)  13.1 us
  transfers between devices with their start and end apart: 5, of which 4 were waited for; matrix products, arithmetic and copies ran while one was open for 2% of the time, Pallas kernels for 0%

profile of v1, /device:TPU:0, one launch (start us, length us, event | category | flops | bytes accessed | tf_op | source)
XLA Modules:
  0.0 493.3 jit_solution(16121326881660455574)
XLA Ops:
  7.2 6.3 %all-to-all-start = ((f32[4,2,256,128]{3,2,1,0:T(8,128)}), f32[4,2,256,128]{3,2,1,0:T(8,128)S(1)}, u32[]{:S(2)}, u32[]{:S(2)}) async-start(f32[4,2,256,128]{3,2,1,0:T(8,128)} %param.9), calls=%async_computation | async-start | bytes 2097152 | tf_op jit(solution)/shard_map/all_to_all | solution.py:334
  13.5 4.9 copy.20
  18.4 20.8 %all-to-all-done = f32[4,2,256,128]{3,2,1,0:T(8,128)S(1)} async-done(((f32[4,2,256,128]{3,2,1,0:T(8,128)}), f32[4,2,256,128]{3,2,1,0:T(8,128)S(1)}, u32[]{:S(2)}, u32[]{:S(2)}) %all-to-all-start) | async-done | bytes 1048608 | tf_op jit(solution)/shard_map/all_to_all | solution.py:334
  39.2 0.0 copy-start.1
  39.2 0.0 copy-start.2
  39.2 0.0 copy-start.3
  39.2 0.0 copy-start.4
  39.2 3.8 all-to-all-start.1
  43.0 0.0 all-reduce.4.cloned.1.call-start
  43.1 0.0 copy-done.1
  43.1 0.0 copy-done.2
  43.1 0.0 copy-done.3
  43.1 58.6 %all_gather.3 = s32[3,1024]{1,0:T(4,128)S(1)} all-gather(s32[3,256]{1,0:T(4,128)S(1)} %pad_add_fusion), channel_id=1, replica_groups=mesh['scan'=2,'slab'=4,'coil'=4] {'slab'}, dimensions={1}, use_global_device_ids=true | all-gather | bytes 15360 | tf_op jit(solution)/shard_map/all_gather | solution.py:337
  101.7 0.7 fusion.11
  102.4 0.0 copy-done.4
  102.4 0.1 select_reduce_fusion
  102.5 1.1 fusion.3.weight
  103.6 1.0 copy.19
  104.7 0.0 all-to-all-done.1
  104.7 1.7 copy.21
  106.4 13.1 %shard_map.95 = f32[2,2,3,128,384]{4,3,2,1,0:T(8,128)} custom-call(f32[2,1024,128]{2,1,0:T(8,128)} %bitcast.27, f32[1024,128]{1,0:T(8,128)} %fusion.3.weight, f32[128,128]{1,0:T(8,128)} %kernel.5, s32[1,1024]{1,0:T(1,128)} %get-tuple-element.12.column, bf16[3,4,2,256,256]{4,3,2,1,0:T(8,128)(2,1)} %constant.75.clone.tables, f32[2,2,3,128,384]{4,3,2,1,0:T(8,128)} %bitcast.22), custom_call_target="tpu_custom_call" | custom-call | tf_op jit(solution)/shard_map/pallas_call | solution.py:356
  119.6 0.0 all-reduce.4.cloned.1.call-update
  119.6 0.2 all-reduce.6.cloned.1.call-start
  119.8 0.9 fusion.4.weight
  120.7 98.3 %all-reduce.4.cloned.1.call-done.image = f32[2,2,3,128,384]{4,3,2,1,0:T(8,128)} async-done(((f32[2,2,3,128,384]{4,3,2,1,0:T(8,128)}), f32[2,2,3,128,384]{4,3,2,1,0:T(8,128)}) %all-reduce.4.cloned.1.call-update) | async-done | bytes 2359312 | tf_op jit(solution)/shard_map/psum | solution.py:354
  218.9 23.7 %shard_map.96 = f32[2,2,3,128,384]{4,3,2,1,0:T(8,128)} custom-call(f32[2,2,3,128,384]{4,3,2,1,0:T(8,128)} %all-reduce.4.cloned.1.call-done.image, f32[128,1024]{1,0:T(8,128)} %fusion.4.weight, f32[128,128]{1,0:T(8,128)} %kernel.5, s32[1,1024]{1,0:T(1,128)} %get-tuple-element.12.column, bf16[3,4,2,256,256]{4,3,2,1,0:T(8,128)(2,1)} %constant.75.clone.tables, ...), custom_call_target="tpu_custom_call" | custom-call | tf_op jit(solution)/shard_map/pallas_call | solution.py:363
  242.6 0.0 copy-start
  242.6 0.0 all-reduce.6.cloned.1.call-update
  242.7 0.3 all-reduce.8.cloned.1.call-start
  242.9 98.1 %all-reduce.6.cloned.1.call-done = f32[2,2,3,128,384]{4,3,2,1,0:T(8,128)} async-done(((f32[2,2,3,128,384]{4,3,2,1,0:T(8,128)}), f32[2,2,3,128,384]{4,3,2,1,0:T(8,128)}) %all-reduce.6.cloned.1.call-update) | async-done | bytes 2359312 | tf_op jit(solution)/shard_map/psum | solution.py:354
  341.1 0.0 copy-done
  341.1 2.9 multiply_reduce_fusion.2
  345.2 4.3 multiply_reduce_fusion.1
  350.8 3.4 multiply_add_fusion.1.image
  354.1 23.7 %shard_map.97 = f32[2,2,3,128,384]{4,3,2,1,0:T(8,128)} custom-call(f32[2,2,3,128,384]{4,3,2,1,0:T(8,128)} %multiply_add_fusion.1.image, f32[128,1024]{1,0:T(8,128)} %fusion.4.weight, f32[128,128]{1,0:T(8,128)} %kernel.5, s32[1,1024]{1,0:T(1,128)} %get-tuple-element.12.column, bf16[3,4,2,256,256]{4,3,2,1,0:T(8,128)(2,1)} %constant.75.clone.tables, ...), custom_call_target="tpu_custom_call" | custom-call | tf_op jit(solution)/shard_map/pallas_call | solution.py:363
  377.8 0.0 all-reduce.8.cloned.1.call-update
  377.8 98.4 %all-reduce.8.cloned.1.call-done = f32[2,2,3,128,384]{4,3,2,1,0:T(8,128)} async-done(((f32[2,2,3,128,384]{4,3,2,1,0:T(8,128)}), f32[2,2,3,128,384]{4,3,2,1,0:T(8,128)}) %all-reduce.8.cloned.1.call-update) | async-done | bytes 2359312 | tf_op jit(solution)/shard_map/psum | solution.py:354
  476.2 5.0 %multiply_add_fusion = (f32[2,2,3,128,384]{4,3,2,1,0:T(8,128)}, f32[]{:T(128)}) fusion(f32[2,2,3,128,384]{4,3,2,1,0:T(8,128)} %all-reduce.8.cloned.1.call-done, f32[2,2,3,128,384]{4,3,2,1,0:T(8,128)} %multiply_add_fusion.1.image), kind=kLoop, calls=%fused_computation.1 | loop fusion | flops 2359295 | bytes 7077892 | tf_op jit(solution)/shard_map/add | solution.py:363
  482.5 1.6 fusion
  484.1 0.5 copy.22
  484.6 0.9 copy.24
  485.4 0.5 copy.23
  485.9 0.9 copy.25
  (1 shorter events, 0.0 us)
Async XLA Ops:
  7.2 32.1 %all-to-all-start = ((f32[4,2,256,128]{3,2,1,0:T(8,128)}), f32[4,2,256,128]{3,2,1,0:T(8,128)S(1)}, u32[]{:S(2)}, u32[]{:S(2)}) async-start(f32[4,2,256,128]{3,2,1,0:T(8,128)} %param.9), calls=%async_computation | async-start | bytes 2097152 | tf_op jit(solution)/shard_map/all_to_all | solution.py:334
  39.2 3.8 copy-start.1
  39.2 3.9 copy-start.2
  39.2 3.9 copy-start.3
  39.2 63.2 %copy-start.4 = (f32[16]{0:T(128)S(1)}, f32[16]{0:T(128)}, u32[]{:S(2)}) copy-start(f32[16]{0:T(128)} %param.14) | copy-start | bytes 196
  39.2 65.5 %all-to-all-start.1 = ((f32[4,2,2,3,32,384]{5,2,3,4,1,0:T(2,128)}), f32[4,2,2,3,32,384]{5,2,3,4,1,0:T(2,128)S(1)}, u32[]{:S(2)}, u32[]{:S(2)}) async-start(f32[4,2,2,3,32,384]{5,2,3,4,1,0:T(2,128)} %bitcast.26), calls=%async_computation.1 | async-start | bytes 4718592 | tf_op jit(solution)/shard_map/all_to_all | solution.py:333
  43.0 175.9 %all-reduce.4.cloned.1.call-start = ((), (), s32[]{:S(2)}) async-start(), calls=%async_computation.2 | async-start | bytes 4718592 | tf_op jit(solution)/shard_map/psum | solution.py:354
  119.6 221.5 %all-reduce.6.cloned.1.call-start = ((), (), s32[]{:S(2)}) async-start(), calls=%async_computation.3 | async-start | bytes 4718592 | tf_op jit(solution)/shard_map/psum | solution.py:354
  242.6 98.4 %copy-start = (f32[2,2,3,128,384]{4,3,2,1,0:T(8,128)S(1)}, f32[2,2,3,128,384]{4,3,2,1,0:T(8,128)}, u32[]{:S(2)}) copy-start(f32[2,2,3,128,384]{4,3,2,1,0:T(8,128)} %all-reduce.4.cloned.1.call-done.image) | copy-start | bytes 7077892
  242.7 233.5 %all-reduce.8.cloned.1.call-start = ((), (), s32[]{:S(2)}) async-start(), calls=%async_computation.4 | async-start | bytes 4718592 | tf_op jit(solution)/shard_map/psum | solution.py:354
Sparse Core Ops, SparseCore 0:
  119.7 99.1 all-reduce.3
  242.8 98.2 all-reduce.5
  377.9 98.2 all-reduce.7

commit v2 on v1

--- a/solution.py
+++ b/solution.py
@@ -168,7 +168,7 @@
 
 
 def mark_blocks(column_ref, marks):
-    step = 256
+    step = 128
     tiles = column_ref.shape[1]
 
     def fill(chunk, carry):
@@ -181,7 +181,7 @@
 
 
 def add_blocks(back_high, back_low, marks, grid):
-    step = 768
+    step = 384
 
     def chunk(index, carry):
         start = pl.multiple_of(index * step, step)
@@ -194,76 +194,78 @@
 
 
 def grid_to_image(grid, tables, middle, maps, out):
-    xpos, _, base, length = maps.shape[1:]
-    span = xpos * length
-    for x in range(xpos):
-        lanes = slice(x * length, (x + 1) * length)
+    coils, _, _, base, length = maps.shape
+    for c in range(coils):
         parts = []
         for q in range(RADIX):
-            part = grid[:, q * span + x * length : q * span + (x + 1) * length]
+            part = grid[2 * base * c : 2 * base * (c + 1), q * length : (q + 1) * length]
             parts.append((part[:base], part[base:]))
         for b, (re, im) in enumerate(butterfly(parts, 1.0)):
             value = jnp.concatenate((re, im), 0)
-            middle[b, :, lanes] = dot_left(tables[b, 1, 0], tables[b, 1, 1], value)
-
-    def rows(index, carry):
-        x, b = index // RADIX, index % RADIX
-        parts = []
-        for r in range(RADIX):
-            start = pl.multiple_of(x * length + r * base, base)
-            value = middle[b, :, pl.ds(start, base)]
-            value = jnp.concatenate((value[:base], value[base:]), 1)
-            back = dot_right(value, tables[r, 3, 0], tables[r, 3, 1])
-            parts.append((back[:, :base], back[:, base:]))
-        for q, (re, im) in enumerate(butterfly(parts, 1.0)):
-            lanes = slice(q * base, (q + 1) * base)
-            map_r, map_i = maps[0, x, b, :, lanes], maps[1, x, b, :, lanes]
-            out[0, x, b, :, lanes] = map_r * re + map_i * im
-            out[1, x, b, :, lanes] = map_r * im - map_i * re
-        return carry
-
-    lax.fori_loop(0, xpos * RADIX, rows, 0)
-
-
-def image_to_grid(image, tables, middle, maps, grid_high, grid_low):
-    xpos, _, base, length = maps.shape[1:]
-    span = xpos * length
-
-    def rows(index, carry):
-        x, b = index // RADIX, index % RADIX
-        parts = []
+            middle[b, :, c * length : (c + 1) * length] = dot_left(tables[b, 1, 0], tables[b, 1, 1], value)
+
+    def rows(b, carry):
+        sums = [None] * RADIX
+        for c in range(coils):
+            parts = []
+            for r in range(RADIX):
+                start = c * length + r * base
+                value = middle[b, :, start : start + base]
+                value = jnp.concatenate((value[:base], value[base:]), 1)
+                back = dot_right(value, tables[r, 3, 0], tables[r, 3, 1])
+                parts.append((back[:, :base], back[:, base:]))
+            for q, (re, im) in enumerate(butterfly(parts, 1.0)):
+                lanes = slice(q * base, (q + 1) * base)
+                map_r, map_i = maps[c, 0, b, :, lanes], maps[c, 1, b, :, lanes]
+                term = (map_r * re + map_i * im, map_r * im - map_i * re)
+                if c:
+                    term = (sums[q][0] + term[0], sums[q][1] + term[1])
+                sums[q] = term
         for q in range(RADIX):
             lanes = slice(q * base, (q + 1) * base)
-            map_r, map_i = maps[0, x, b, :, lanes], maps[1, x, b, :, lanes]
-            re, im = image[0, x, b, :, lanes], image[1, x, b, :, lanes]
-            parts.append((map_r * re - map_i * im, map_r * im + map_i * re))
-        for r, (re, im) in enumerate(butterfly(parts, -1.0)):
-            value = dot_right(jnp.concatenate((re, im), 1), tables[r, 2, 0], tables[r, 2, 1])
-            start = pl.multiple_of(x * length + r * base, base)
-            middle[b, :base, pl.ds(start, base)] = value[:, :base]
-            middle[b, base:, pl.ds(start, base)] = value[:, base:]
+            out[0, b, :, lanes], out[1, b, :, lanes] = sums[q]
         return carry
 
-    lax.fori_loop(0, xpos * RADIX, rows, 0)
-    for x in range(xpos):
+    lax.fori_loop(0, RADIX, rows, 0)
+
+
+def image_to_grid(image, tables, middle, maps, grid_high, grid_low):
+    coils, _, _, base, length = maps.shape
+
+    def rows(b, carry):
+        for c in range(coils):
+            parts = []
+            for q in range(RADIX):
+                lanes = slice(q * base, (q + 1) * base)
+                map_r, map_i = maps[c, 0, b, :, lanes], maps[c, 1, b, :, lanes]
+                re, im = image[0, b, :, lanes], image[1, b, :, lanes]
+                parts.append((map_r * re - map_i * im, map_r * im + map_i * re))
+            for r, (re, im) in enumerate(butterfly(parts, -1.0)):
+                value = dot_right(jnp.concatenate((re, im), 1), tables[r, 2, 0], tables[r, 2, 1])
+                start = c * length + r * base
+                middle[b, :base, start : start + base] = value[:, :base]
+                middle[b, base:, start : start + base] = value[:, base:]
+        return carry
+
+    lax.fori_loop(0, RADIX, rows, 0)
+    for c in range(coils):
         parts = []
         for b in range(RADIX):
-            value = middle[b, :, x * length : (x + 1) * length]
+            value = middle[b, :, c * length : (c + 1) * length]
             value = dot_left(tables[b, 0, 0], tables[b, 0, 1], value)
             parts.append((value[:base], value[base:]))
         for q, (re, im) in enumerate(butterfly(parts, -1.0)):
             high, low = split(jnp.concatenate((re, im), 0))
-            lanes = slice(q * span + x * length, q * span + (x + 1) * length)
-            grid_high[:, lanes] = high
-            grid_low[:, lanes] = low
+            rows_c, lanes = slice(2 * base * c, 2 * base * (c + 1)), slice(q * length, (q + 1) * length)
+            grid_high[rows_c, lanes] = high
+            grid_low[rows_c, lanes] = low
 
 
 def rhs_kernel(samples, weight, kernel, column, tables, maps, out, marks, back_high, back_low, middle, grid):
     base = kernel.shape[0]
     mark_blocks(column, marks)
-    kernel_t = kernel[...].T
-    kernel_high, kernel_low = split(kernel_t)
-    for part in range(2):
+    kernel_high, kernel_low = split(kernel[...].T)
+    for part in range(samples.shape[0]):
         value = samples[part] * weight[...]
         back = dot_left(kernel_high, kernel_low, value, ((1,), (1,)))
         high, low = split(back)
@@ -285,7 +287,7 @@
         start = pl.multiple_of(index * step, step)
         mark = marks[:, pl.ds(start, step)]
         picked = dot(grid_high[...], mark) + dot(grid_low[...], mark)
-        for part in range(2):
+        for part in range(picked.shape[0] // base):
             rows = slice(part * base, (part + 1) * base)
             value = dot_left(kernel_high, kernel_low, picked[rows]) * weight[:, pl.ds(start, step)]
             high, low = split(dot_left(turned_high, turned_low, value))
@@ -298,25 +300,195 @@
     grid_to_image(grid, tables, middle, maps, out)
 
 
-def call(kernel, image_shape, tiles, forward):
-    base, length = image_shape[-2:]
-    cells = image_shape[1] * RADIX * length
+def call(kernel, map_shape, tiles, forward):
+    coils, _, _, base, length = map_shape
+    cells = RADIX * length
+    rows = 2 * base * coils
     scratch = [
         pltpu.VMEM((cells, tiles), BF16),
-        pltpu.VMEM((2 * base, tiles), BF16),
-        pltpu.VMEM((2 * base, tiles), BF16),
-        pltpu.VMEM((RADIX, 2 * base, image_shape[1] * length), F32),
-        pltpu.VMEM((2 * base, cells), F32),
+        pltpu.VMEM((rows, tiles), BF16),
+        pltpu.VMEM((rows, tiles), BF16),
+        pltpu.VMEM((RADIX, 2 * base, coils * length), F32),
+        pltpu.VMEM((rows, cells), F32),
     ]
     if forward:
-        scratch += [pltpu.VMEM((2 * base, cells), BF16)] * 2
+        scratch += [pltpu.VMEM((rows, cells), BF16)] * 2
     return pl.pallas_call(
         kernel,
-        out_shape=jax.ShapeDtypeStruct(image_shape, F32),
+        out_shape=jax.ShapeDtypeStruct(map_shape[1:], F32),
         in_specs=[pl.BlockSpec(memory_space=pltpu.VMEM)] * 6,
         out_specs=pl.BlockSpec(memory_space=pltpu.VMEM),
         scratch_shapes=scratch,
         compiler_params=pltpu.CompilerParams(vmem_limit_bytes=56 * 2**20),
+    )
+
+
+CHUNKS = 4
+STEP = 96
+
+
+def combine(first, refs):
+    if first:
+        part, direction_out, norm_out, whole, landed, work, tile, send, recv = refs
+    else:
+        (part, direction, residual, answer, norm, direction_out, residual_out, answer_out, norm_out,
+         whole, landed, work, tile, send, recv) = refs
+    slab, coil = lax.axis_index("slab"), lax.axis_index("coil")
+    core, chip, far, near = coil % 2, coil // 2, slab // 2, slab % 2
+    partners = (
+        {"coil": chip * 2 + (1 - core)},
+        {"coil": (1 - chip) * 2 + core},
+        {"slab": (1 - far) * 2 + near},
+        {"slab": far * 2 + (1 - near)},
+    )
+    bits = (core, chip, far)
+    barrier = pltpu.get_barrier_semaphore()
+    for partner in partners:
+        pl.semaphore_signal(barrier, inc=1, device_id=partner, device_id_type=pl.DeviceIdType.MESH)
+    pl.semaphore_wait(barrier, len(partners))
+
+    total = part.shape[0]
+    size = total // CHUNKS
+    sent = []
+
+    def rows(start, count):
+        return pl.ds(pl.multiple_of(start, 8), count)
+
+    def push(source, target, slot, axis):
+        copy = pltpu.make_async_remote_copy(
+            src_ref=source,
+            dst_ref=target,
+            send_sem=send.at[slot],
+            recv_sem=recv.at[slot],
+            device_id=partners[axis],
+            device_id_type=pl.DeviceIdType.MESH,
+        )
+        copy.start()
+        sent.append(copy)
+        return copy
+
+    orders = [(0, 1, 2) if chunk % 2 == 0 else (0, 2, 1) for chunk in range(CHUNKS)]
+    starts = [chunk * size for chunk in range(CHUNKS)]
+    flying = [None] * CHUNKS
+    place = [0, size // 2, size // 2 + size // 4]
+    slots = [[None] * 3 for _ in range(CHUNKS)]
+    for stage in range(4):
+        for chunk in range(CHUNKS):
+            count = size >> stage
+            if stage:
+                flying[chunk].wait_recv()
+                mine = rows(starts[chunk], count)
+                arrived = landed[chunk, place[stage - 1] : place[stage - 1] + count, :]
+                held = part if stage == 1 else work
+                goal = whole if stage == 3 else work
+                goal[mine, :] = held[mine, :] + arrived
+            if stage < 3:
+                half = count // 2
+                bit = bits[orders[chunk][stage]]
+                other = starts[chunk] + (1 - bit) * half
+                source = part if stage == 0 else work
+                target = landed.at[chunk, pl.ds(place[stage], half), :]
+                flying[chunk] = push(source.at[rows(other, half), :], target, chunk * 6 + stage, orders[chunk][stage])
+                starts[chunk] = starts[chunk] + bit * half
+    for stage in range(4):
+        for chunk in range(CHUNKS):
+            if stage:
+                flying[chunk].wait_recv()
+                axis = orders[chunk][3 - stage]
+                starts[chunk] = starts[chunk] - bits[axis] * (size >> (4 - stage))
+            if stage < 3:
+                axis = orders[chunk][2 - stage]
+                mine = whole.at[rows(starts[chunk], size >> (3 - stage)), :]
+                flying[chunk] = push(mine, mine, chunk * 6 + 3 + stage, axis)
+
+    for copy in sent:
+        copy.wait_send()
+    sent.clear()
+
+    def exchange(value, index):
+        tile[index, 0] = jnp.broadcast_to(value, tile.shape[2:])
+        copy = push(tile.at[index, 0], tile.at[index, 1], CHUNKS * 6 + index, 3)
+        copy.wait_recv()
+        return (tile[index, 0] + tile[index, 1])[:1, :1]
+
+    def sweep(body):
+        def step(index, carry):
+            return carry + body(rows(index * STEP, STEP))
+
+        lanes = lax.fori_loop(0, total // STEP, step, jnp.zeros((8, part.shape[1]), F32))
+        return jnp.sum(lanes, keepdims=True)
+
+    def fold(value):
+        return jnp.sum(value.reshape(-1, 8, value.shape[1]), 0)
+
+    if first:
+
+        def copy_out(at):
+            value = whole[at, :]
+            direction_out[at, :] = value
+            return fold(value * value)
+
+        norm_out[...] = jnp.broadcast_to(exchange(sweep(copy_out), 0), norm_out.shape)
+    else:
+
+        def meet(at):
+            move = direction[at, :]
+            image = whole[at, :] + SHIFT * move
+            work[at, :] = image
+            return fold(move * image)
+
+        before = norm[:1, :1]
+        alpha = before / exchange(sweep(meet), 0)
+
+        def shrink(at):
+            left = residual[at, :] - alpha * work[at, :]
+            residual_out[at, :] = left
+            answer_out[at, :] = answer[at, :] + alpha * direction[at, :]
+            return fold(left * left)
+
+        after = exchange(sweep(shrink), 1)
+        beta = after / before
+
+        def turn(index, carry):
+            at = rows(index * STEP, STEP)
+            direction_out[at, :] = residual_out[at, :] + beta * direction[at, :]
+            return carry
+
+        lax.fori_loop(0, total // STEP, turn, 0)
+        norm_out[...] = jnp.broadcast_to(after, norm_out.shape)
+    for copy in sent:
+        copy.wait_send()
+
+
+def first_kernel(*refs):
+    combine(True, refs)
+
+
+def next_kernel(*refs):
+    combine(False, refs)
+
+
+def combine_call(first, shape):
+    image = jax.ShapeDtypeStruct(shape, F32)
+    scalar = jax.ShapeDtypeStruct((8, 128), F32)
+    copies = CHUNKS * 6 + 2
+    memory = pl.BlockSpec(memory_space=pltpu.VMEM)
+    return pl.pallas_call(
+        first_kernel if first else next_kernel,
+        out_shape=(image, scalar) if first else (image, image, image, scalar),
+        in_specs=[memory] * (1 if first else 5),
+        out_specs=[memory] * (2 if first else 4),
+        scratch_shapes=[
+            pltpu.VMEM(shape, F32),
+            pltpu.VMEM((CHUNKS, shape[0] // CHUNKS, shape[1]), F32),
+            pltpu.VMEM(shape, F32),
+            pltpu.VMEM((2, 2, 8, 128), F32),
+            pltpu.SemaphoreType.DMA((copies,)),
+            pltpu.SemaphoreType.DMA((copies,)),
+        ],
+        compiler_params=pltpu.CompilerParams(
+            collective_id=0 if first else 1, has_side_effects=True, vmem_limit_bytes=56 * 2**20
+        ),
     )
 
 
@@ -328,10 +500,15 @@
     ky_dev = ylen // slabs
     lines = zdev // RADIX
     zblocks = zdev * slabs // base
-
-    near = coil_maps.reshape(ncoil, 2, xpos, lines, RADIX, ylen).transpose(0, 1, 2, 4, 3, 5)
+    pairs = slabs // xpos
+    group = ncoil // pairs
+
+    near = coil_maps.reshape(pairs, group, 2, xpos, lines, RADIX, ylen).transpose(0, 3, 1, 2, 5, 4, 6)
+    near = near.reshape(slabs, group, 2, RADIX, lines, ylen)
+    data = samples.reshape(pairs, 1, group * 2, *samples.shape[2:])
+    data = jnp.broadcast_to(data, (pairs, xpos, *data.shape[2:])).reshape(slabs, *data.shape[2:])
+    data = lax.all_to_all(data, "slab", split_axis=0, concat_axis=2, tiled=True)[0]
     maps = lax.all_to_all(near, "slab", split_axis=0, concat_axis=4, tiled=True)[0]
-    data = lax.all_to_all(samples, "slab", split_axis=0, concat_axis=2, tiled=True)[0]
 
     cells = jnp.stack((tile_block, tile_count, dcf_level))
     cells = lax.all_gather(cells, "slab", axis=1, tiled=True)
@@ -339,8 +516,8 @@
     tiles = block.shape[0]
     shard = jnp.arange(tiles, dtype=jnp.int32) // (tiles // slabs)
     ky = shard * ky_dev + block // zblocks % ky_dev
-    column = (block % zblocks * xpos + block // (zblocks * ky_dev)) * ylen
-    column = (column + ky % RADIX * base + ky // RADIX)[None, :]
+    column = block % zblocks * ylen + ky % RADIX * base + ky // RADIX
+    column = jnp.where(block // (zblocks * ky_dev) == slab % xpos, column, -1)[None, :]
     levels = jnp.arange(dcf_table.shape[0], dtype=jnp.int32)
     density = jnp.sum(jnp.where(level[:, None] == levels[None, :], dcf_table[None, :], 0.0), axis=1)
     position = jnp.arange(base, dtype=jnp.int32)
@@ -349,30 +526,26 @@
 
     tables = jnp.asarray(dft_tables(ylen))
     shape = maps.shape
-
-    def total(local):
-        return lax.psum(local, ("slab", "coil"))
-
-    rhs = total(call(rhs_kernel, shape, tiles, False)(data, weight, kernel, column, tables, maps))
-    solution = jnp.zeros_like(rhs)
-    residual = rhs
-    direction = rhs
-    norm_now = jnp.sum(residual * residual)
+    flat = (2 * RADIX * base, ylen)
+
+    partial = call(rhs_kernel, shape, tiles, False)(data, weight, kernel, column, tables, maps)
+    direction, norm = combine_call(True, flat)(partial.reshape(flat))
+    residual, answer = direction, jnp.zeros_like(direction)
     normal = call(normal_kernel, shape, tiles, True)
+    update = combine_call(False, flat)
     for step in range(ITERS):
-        image = total(normal(direction, weight_t, kernel, column, tables, maps)) + SHIFT * direction
-        alpha = norm_now / jnp.sum(direction * image)
-        solution = solution + alpha * direction
-        residual = residual - alpha * image
-        norm_next = jnp.sum(residual * residual)
-        direction = residual + norm_next / norm_now * direction
-        norm_now = norm_next
-
-    def own(value):
-        piece = lax.dynamic_slice_in_dim(value, slab * lines, lines, 3)
-        return piece.transpose(0, 1, 3, 2, 4).reshape(2, xpos, zdev, ylen)
-
-    return own(solution), own(residual)
+        partial = normal(direction.reshape(shape[1:]), weight_t, kernel, column, tables, maps)
+        direction, residual, answer, norm = update(partial.reshape(flat), direction, residual, answer, norm)
+
+    both = jnp.stack((answer, residual)).reshape(2, 2, RADIX, base, ylen)
+    partner = slab + 1 - 2 * (slab % 2)
+    keep = lax.dynamic_slice_in_dim(both, slab * lines, lines, 3)
+    give = lax.dynamic_slice_in_dim(both, partner * lines, lines, 3)
+    take = lax.ppermute(give, "slab", [(index, index ^ 1) for index in range(slabs)])
+    low = slab % 2 == 0
+    both = jnp.stack((jnp.where(low, keep, take), jnp.where(low, take, keep)), 2)
+    both = both.transpose(0, 1, 2, 4, 3, 5).reshape(2, 2, xpos, zdev, ylen)
+    return both[0], both[1]
 
 
 def fits(mesh, coil_maps, samples, kernel):
@@ -381,7 +554,8 @@
     zlen, ylen = coil_maps.shape[3:]
     base = kernel.shape[0]
     return (
-        coil_dev == slabs
+        coil_dev == slabs == coils == 4
+        and coil_maps.shape[2] == 2
         and zlen == ylen == RADIX * base
         and base == 128
         and zlen % (slabs * RADIX) == 0

time: 494 us -> 323 us (0.65)
  waiting for transfers between devices: 316 us -> 56.8 us
  Pallas kernels: 60.5 us -> 174 us
  between operations: 17.7 us -> 0.81 us
  other arithmetic: 19.9 us -> 4.27 us
  local copies, waits for them, and re-layouts: 10.3 us -> 18.1 us
    psum x3 -> x0, waiting for transfers between devices: 295 us -> none  [total(): return lax.psum(local, ('slab', 'coil'))]
    pallas_call x2 -> x5, Pallas kernels: 47.4 us -> 161 us  [the longest x2 77.6 us: whole_coils(): update(partial.reshape(flat), direction, residual, answer, norm)]
    all_to_all x1, waiting for transfers between devices: 20.8 us -> 42.9 us  [whole_coils(): lax.all_to_all(data, 'slab', split_axis=0, concat_axis=2, tiled=True)[0]]
    ppermute x0 -> x1, waiting for transfers between devices: none -> 13.9 us  [whole_coils(): lax.ppermute(give, 'slab', [(index, index ^ 1) for index in range(slabs)])]
    add x3 -> x0, other arithmetic: 9.04 us -> none  [the longest x1 4.96 us: whole_coils(): total(normal(direction, weight_t, kernel, column, tables, maps))]
    reduce_sum x2 -> x0, other arithmetic: 7.17 us -> none  [the longest x1 4.26 us: whole_coils(): norm_next = jnp.sum(residual * residual)]
  transfers between devices with their start and end apart: 5 -> 3, of which waited for: 4 -> 2; matrix products, arithmetic and copies ran while one was open for 2% -> 3% of each run, Pallas kernels for 0% -> 0%
where the time goes in v2:
time: 323 us; the launch traced here: 322 us
  Pallas kernels  174 us (54%)
  blocking collectives  58.6 us (18%)
  waiting for transfers between devices  56.8 us (18%)
  local copies, waits for them, and re-layouts  18.1 us (6%)
  starting transfers between devices  10 us (3%)
  other arithmetic  4.27 us (1%)
    pallas_call x2, Pallas kernels, whole_coils(): update(partial.reshape(flat), direction, residual, answer, norm)  77.6 us
    all_gather x1, blocking collectives, whole_coils(): cells = lax.all_gather(cells, 'slab', axis=1, tiled=True)  58.6 us
    pallas_call x2, Pallas kernels, whole_coils(): normal(direction.reshape(shape[1:]), weight_t, kernel, column, tables, maps)  50.9 us
    all_to_all x1, waiting for transfers between devices, whole_coils(): lax.all_to_all(data, 'slab', split_axis=0, concat_axis=2, tiled=True)[0]  42.9 us
    pallas_call x1, Pallas kernels, whole_coils(): direction, norm = combine_call(True, flat)(partial.reshape(flat))  32.2 us
    ppermute x1, waiting for transfers between devices, whole_coils(): lax.ppermute(give, 'slab', [(index, index ^ 1) for index in range(slabs)])  13.9 us
    pallas_call x1, Pallas kernels, whole_coils(): call(rhs_kernel, shape, tiles, False)  13 us
    unnamed x17, local copies, waits for them, and re-layouts  6.58 us
  transfers between devices with their start and end apart: 3, of which 2 were waited for; matrix products, arithmetic and copies ran while one was open for 3% of the time, Pallas kernels for 0%

profile of v2, /device:TPU:0, one launch (start us, length us, event | category | flops | bytes accessed | tf_op | source)
XLA Modules:
  0.0 322.2 jit_solution(9855056680511131594)
XLA Ops:
  0.6 2.8 broadcast_in_dim.56
  3.4 6.3 %all-to-all-start = ((f32[4,4,256,128]{3,2,1,0:T(8,128)}), f32[4,4,256,128]{3,2,1,0:T(8,128)S(1)}, u32[]{:S(2)}, u32[]{:S(2)}) async-start(f32[4,4,256,128]{3,2,1,0:T(8,128)} %bitcast.41), calls=%async_computation | async-start | bytes 4194304 | tf_op jit(solution)/shard_map/all_to_all | solution.py:510
  9.7 3.5 %copy.38 = f32[4,2,2,96,384]{4,2,3,1,0:T(2,128)S(1)} copy(f32[4,2,2,96,384]{4,3,2,1,0:T(8,128)} %param.8) | data formatting | bytes 4718592 | tf_op args[0]
  13.2 1.8 copy.39
  15.0 42.9 %all-to-all-done = f32[4,4,256,128]{3,2,1,0:T(8,128)S(1)} async-done(((f32[4,4,256,128]{3,2,1,0:T(8,128)}), f32[4,4,256,128]{3,2,1,0:T(8,128)S(1)}, u32[]{:S(2)}, u32[]{:S(2)}) %all-to-all-start) | async-done | bytes 2097184 | tf_op jit(solution)/shard_map/all_to_all | solution.py:510
  57.9 0.0 copy-start
  57.9 0.0 copy-start.3
  57.9 0.0 copy-start.4
  57.9 0.0 copy-start.5
  57.9 0.0 copy-start.6
  58.0 1.3 copy-done
  59.3 3.6 %all-to-all-start.1 = ((f32[4,2,2,3,32,384]{5,4,3,2,1,0:T(8,128)}), f32[4,2,2,3,32,384]{5,4,3,2,1,0:T(8,128)S(1)}, u32[]{:S(2)}, u32[]{:S(2)}) async-start(f32[4,2,2,3,32,384]{5,4,3,2,1,0:T(8,128)} %bitcast.12), calls=%async_computation.1 | async-start | bytes 4718592 | tf_op jit(solution)/shard_map/all_to_all | solution.py:511
  63.0 0.0 copy-done.3
  63.0 0.0 copy-done.4
  63.0 0.0 copy-done.5
  63.0 58.6 %all_gather.3 = s32[3,1024]{1,0:T(4,128)S(1)} all-gather(s32[3,256]{1,0:T(4,128)S(1)} %pad_add_fusion), channel_id=1, replica_groups=mesh['scan'=2,'slab'=4,'coil'=4] {'slab'}, dimensions={1}, use_global_device_ids=true | all-gather | bytes 15360 | tf_op jit(solution)/shard_map/all_gather | solution.py:514
  121.6 0.7 compare_select_fusion
  122.4 0.0 copy-done.6
  122.4 0.1 select_reduce_fusion
  122.4 1.1 fusion.2.weight
  123.6 0.9 fusion.3.weight
  124.4 3.1 copy.37
  127.5 0.0 all-to-all-done.1
  127.5 1.6 copy.40
  129.2 13.0 %shard_map.95 = f32[2,3,128,384]{3,2,1,0:T(8,128)} custom-call(f32[4,1024,128]{2,1,0:T(8,128)} %bitcast.42, f32[1024,128]{1,0:T(8,128)} %fusion.2.weight, f32[128,128]{1,0:T(8,128)} %kernel.5, s32[1,1024]{1,0:T(1,128)} %get-tuple-element.30.column, bf16[3,4,2,256,256]{4,3,2,1,0:T(8,128)(2,1)} %constant.89.clone.tables, f32[2,2,3,128,384]{4,3,2,1,0:T(8,128)} %bitcast.34), custom_call_target="tpu_custom_call" | custom-call | tf_op jit(solution)/shard_map/pallas_call | solution.py:531
  142.2 32.2 %shard_map.96 = (f32[768,384]{1,0:T(8,128)}, f32[8,128]{1,0:T(8,128)}) custom-call(f32[768,384]{1,0:T(8,128)} %bitcast.47), custom_call_target="tpu_custom_call" | custom-call | tf_op jit(solution)/shard_map/pallas_call | solution.py:532
  174.4 25.3 %shard_map.97 = f32[2,3,128,384]{3,2,1,0:T(8,128)} custom-call(f32[2,3,128,384]{3,2,1,0:T(8,128)} %bitcast.37, f32[128,1024]{1,0:T(8,128)} %fusion.3.weight, f32[128,128]{1,0:T(8,128)} %kernel.5, s32[1,1024]{1,0:T(1,128)} %get-tuple-element.30.column, bf16[3,4,2,256,256]{4,3,2,1,0:T(8,128)(2,1)} %constant.89.clone.tables, f32[2,2,3,128,384]{4,3,2,1,0:T(8,128)} %bitcast.35), custom_call_target="tpu_custom_call" | custom-call | tf_op jit(solution)/shard_map/pallas_call | solution.py:537
  199.7 1.2 broadcast_in_dim.63.refs_3_
  200.9 38.8 %shard_map.98 = (f32[768,384]{1,0:T(8,128)}, f32[768,384]{1,0:T(8,128)}, f32[768,384]{1,0:T(8,128)}, f32[8,128]{1,0:T(8,128)}) custom-call(f32[768,384]{1,0:T(8,128)} %bitcast.50, f32[768,384]{1,0:T(8,128)} %get-tuple-element.10.refs_1_.refs_2_, f32[768,384]{1,0:T(8,128)} %get-tuple-element.10.refs_1_.refs_2_, f32[768,384]{1,0:T(8,128)} %broadcast_in_dim.63.refs_3_, ...), custom_call_target="tpu_custom_call" | custom-call | tf_op jit(solution)/shard_map/pallas_call | solution.py:538
  239.6 25.6 %shard_map.99 = f32[2,3,128,384]{3,2,1,0:T(8,128)} custom-call(f32[2,3,128,384]{3,2,1,0:T(8,128)} %bitcast.48, f32[128,1024]{1,0:T(8,128)} %fusion.3.weight, f32[128,128]{1,0:T(8,128)} %kernel.5, s32[1,1024]{1,0:T(1,128)} %get-tuple-element.30.column, bf16[3,4,2,256,256]{4,3,2,1,0:T(8,128)(2,1)} %constant.89.clone.tables, f32[2,2,3,128,384]{4,3,2,1,0:T(8,128)} %bitcast.36), custom_call_target="tpu_custom_call" | custom-call | tf_op jit(solution)/shard_map/pallas_call | solution.py:537
  265.2 38.8 %shard_map.100 = (f32[768,384]{1,0:T(8,128)}, f32[768,384]{1,0:T(8,128)}, f32[768,384]{1,0:T(8,128)}, f32[8,128]{1,0:T(8,128)}) custom-call(f32[768,384]{1,0:T(8,128)} %bitcast.49, f32[768,384]{1,0:T(8,128)} %get-tuple-element.12.refs_1_, f32[768,384]{1,0:T(8,128)} %get-tuple-element.13.refs_2_, f32[768,384]{1,0:T(8,128)} %get-tuple-element.14.refs_3_, ...), custom_call_target="tpu_custom_call" | custom-call | tf_op jit(solution)/shard_map/pallas_call | solution.py:538
  304.0 0.0 copy-start.1
  304.0 0.0 copy-start.2
  304.0 1.3 fusion
  305.3 0.1 collective-permute-start
  305.4 13.9 %collective-permute-done = f32[2,2,3,32,384]{4,3,2,1,0:T(8,128)S(1)} collective-permute-done((f32[2,2,3,32,384]{4,3,2,1,0:T(8,128)S(1)}, f32[2,2,3,32,384]{4,3,2,1,0:T(8,128)S(1)}, u32[]{:S(2)}, u32[]{:S(2)}) %collective-permute-start) | collective-permute-done | bytes 589856 | tf_op jit(solution)/shard_map/ppermute | solution.py:544
  319.2 0.0 copy-done.1
  319.2 0.0 copy-done.2
  319.2 0.1 select_bitcast_fusion.1
  319.4 0.1 maximum_bitcast_fusion
  319.5 0.1 fusion.10
  319.6 0.5 copy.41
  320.1 0.9 copy.43
  320.9 0.5 copy.42
  321.4 0.9 copy.44
  (1 shorter events, 0.0 us)
Async XLA Ops:
  3.4 54.5 %all-to-all-start = ((f32[4,4,256,128]{3,2,1,0:T(8,128)}), f32[4,4,256,128]{3,2,1,0:T(8,128)S(1)}, u32[]{:S(2)}, u32[]{:S(2)}) async-start(f32[4,4,256,128]{3,2,1,0:T(8,128)} %bitcast.41), calls=%async_computation | async-start | bytes 4194304 | tf_op jit(solution)/shard_map/all_to_all | solution.py:510
  57.9 1.4 copy-start
  57.9 5.0 %copy-start.3 = (s32[256]{0:T(256)S(1)}, s32[256]{0:T(256)}, u32[]{:S(2)}) copy-start(s32[256]{0:T(256)} %param.13) | copy-start | bytes 3076
  57.9 5.0 %copy-start.4 = (s32[256]{0:T(256)S(1)}, s32[256]{0:T(256)}, u32[]{:S(2)}) copy-start(s32[256]{0:T(256)} %param.12) | copy-start | bytes 3076
  57.9 5.0 %copy-start.5 = (s32[256]{0:T(256)S(1)}, s32[256]{0:T(256)}, u32[]{:S(2)}) copy-start(s32[256]{0:T(256)} %param.11) | copy-start | bytes 3076
  57.9 64.4 %copy-start.6 = (f32[16]{0:T(128)S(1)}, f32[16]{0:T(128)}, u32[]{:S(2)}) copy-start(f32[16]{0:T(128)} %param.14) | copy-start | bytes 196
  59.3 68.2 %all-to-all-start.1 = ((f32[4,2,2,3,32,384]{5,4,3,2,1,0:T(8,128)}), f32[4,2,2,3,32,384]{5,4,3,2,1,0:T(8,128)S(1)}, u32[]{:S(2)}, u32[]{:S(2)}) async-start(f32[4,2,2,3,32,384]{5,4,3,2,1,0:T(8,128)} %bitcast.12), calls=%async_computation.1 | async-start | bytes 4718592 | tf_op jit(solution)/shard_map/all_to_all | solution.py:511
  304.0 15.2 %copy-start.1 = (f32[768,384]{1,0:T(8,128)S(1)}, f32[768,384]{1,0:T(8,128)}, u32[]{:S(2)}) copy-start(f32[768,384]{1,0:T(8,128)} %get-tuple-element.17) | copy-start | bytes 3538948
  304.0 15.2 %copy-start.2 = (f32[768,384]{1,0:T(8,128)S(1)}, f32[768,384]{1,0:T(8,128)}, u32[]{:S(2)}) copy-start(f32[768,384]{1,0:T(8,128)} %get-tuple-element.16) | copy-start | bytes 3538948
  305.3 14.0 %collective-permute-start = (f32[2,2,3,32,384]{4,3,2,1,0:T(8,128)S(1)}, f32[2,2,3,32,384]{4,3,2,1,0:T(8,128)S(1)}, u32[]{:S(2)}, u32[]{:S(2)}) collective-permute-start(f32[2,2,3,32,384]{4,3,2,1,0:T(8,128)S(1)} %fusion), channel_id=1, source_target_pairs={{0,4},{4,0},{8,12},{12,8},{1,5},{5,1},{9,13},{13,9},{2,6},{6,2},{1... | collective-permute-start | bytes 1769480 | tf_op jit(solution)/shard_map/ppermute | solution.py:544

commit v3 on v2

--- a/solution.py
+++ b/solution.py
@@ -167,17 +167,19 @@
     return np.stack((high, low), 2)
 
 
-def mark_blocks(column_ref, marks):
+def mark_blocks(info, marks):
     step = 128
-    tiles = column_ref.shape[1]
+    cells, tiles = marks.shape
+    offset = (lax.axis_index("slab") % 2 * cells).astype(F32)
+    column = info[0:1, :] - offset
 
     def fill(chunk, carry):
         start = pl.multiple_of(chunk * step, step)
         rows = lax.broadcasted_iota(jnp.int32, (step, tiles), 0) + start
-        marks[pl.ds(start, step), :] = (rows == column_ref[...]).astype(F32).astype(BF16)
+        marks[pl.ds(start, step), :] = (rows.astype(F32) == column).astype(F32).astype(BF16)
         return carry
 
-    lax.fori_loop(0, marks.shape[0] // step, fill, 0)
+    lax.fori_loop(0, cells // step, fill, 0)
 
 
 def add_blocks(back_high, back_low, marks, grid):
@@ -193,7 +195,7 @@
     lax.fori_loop(0, marks.shape[0] // step, chunk, 0)
 
 
-def grid_to_image(grid, tables, middle, maps, out):
+def grid_to_image(grid, tables, middle, maps, out, ready=None):
     coils, _, _, base, length = maps.shape
     for c in range(coils):
         parts = []
@@ -203,6 +205,9 @@
         for b, (re, im) in enumerate(butterfly(parts, 1.0)):
             value = jnp.concatenate((re, im), 0)
             middle[b, :, c * length : (c + 1) * length] = dot_left(tables[b, 1, 0], tables[b, 1, 1], value)
+
+    if ready is not None:
+        ready()
 
     def rows(b, carry):
         sums = [None] * RADIX
@@ -261,23 +266,94 @@
             grid_low[rows_c, lanes] = low
 
 
-def rhs_kernel(samples, weight, kernel, column, tables, maps, out, marks, back_high, back_low, middle, grid):
+def rhs_kernel(near_maps, samples, weight, own_info, kernel, tables, out, maps, info, data, arrived,
+               marks, back_high, back_low, middle, grid, send, recv):
     base = kernel.shape[0]
-    mark_blocks(column, marks)
+    shard_tiles = samples.shape[1]
+    lines = near_maps.shape[4]
+    slab = lax.axis_index("slab")
+    far, near = slab // 2, slab % 2
+    others = ((1 - far) * 2 + near, far * 2 + (1 - near), (1 - far) * 2 + (1 - near))
+    barrier = pltpu.get_barrier_semaphore()
+    for other in others:
+        pl.semaphore_signal(barrier, inc=1, device_id={"slab": other}, device_id_type=pl.DeviceIdType.MESH)
+    pl.semaphore_wait(barrier, len(others))
+
+    sent = []
+
+    def push(source, target, slot, other):
+        copy = pltpu.make_async_remote_copy(
+            src_ref=source,
+            dst_ref=target,
+            send_sem=send.at[slot],
+            recv_sem=recv.at[slot],
+            device_id={"slab": other},
+            device_id_type=pl.DeviceIdType.MESH,
+        )
+        copy.start()
+        sent.append(copy)
+        return copy
+
+    parts = samples.shape[0] // 2
+
+    def tiles_of(shard):
+        return pl.ds(pl.multiple_of(shard * shard_tiles, shard_tiles), shard_tiles)
+
+    def lines_of(shard):
+        return pl.ds(pl.multiple_of(shard * lines, lines), lines)
+
+    mine = tiles_of(slab)
+    info_copies = [push(own_info, arrived.at[slab], index, other) for index, other in enumerate(others)]
+    for part in range(samples.shape[0]):
+        staged_samples = samples[part] * weight[...]
+        data[part // parts, part % parts, mine, :] = staged_samples
+    far_copy = push(data.at[1 - far, :, mine, :], data.at[1 - far, :, mine, :], 3, others[0])
+    near_copy = push(data.at[far, :, mine, :], data.at[far, :, mine, :], 4, others[1])
+    map_copies = []
+    for index in (2, 0, 1):
+        other = others[index]
+        map_copies.append(push(near_maps.at[other], maps.at[:, :, :, lines_of(slab), :], 6 + index, other))
+    maps[:, :, :, lines_of(slab), :] = near_maps[slab]
+    arrived[slab] = own_info[...]
+    for copy in info_copies:
+        copy.wait_recv()
+    for shard in range(arrived.shape[0]):
+        info[:, shard * shard_tiles : (shard + 1) * shard_tiles] = arrived[shard]
+    mark_blocks(info, marks)
+    far_copy.wait_recv()
+    passed = data.at[far, :, tiles_of(others[0]), :]
+    last_copy = push(passed, passed, 5, others[1])
+
     kernel_high, kernel_low = split(kernel[...].T)
-    for part in range(samples.shape[0]):
-        value = samples[part] * weight[...]
-        back = dot_left(kernel_high, kernel_low, value, ((1,), (1,)))
-        high, low = split(back)
-        back_high[part * base : (part + 1) * base, :] = high
-        back_low[part * base : (part + 1) * base, :] = low
+
+    def grid_tiles(shard):
+        at = tiles_of(shard)
+        for part in range(parts):
+            back = dot_left(kernel_high, kernel_low, data[far, part, at, :], ((1,), (1,)))
+            high, low = split(back)
+            back_high[part * base : (part + 1) * base, at] = high
+            back_low[part * base : (part + 1) * base, at] = low
+
+    grid_tiles(slab)
+    grid_tiles(others[0])
+    near_copy.wait_recv()
+    grid_tiles(others[1])
+    last_copy.wait_recv()
+    grid_tiles(others[2])
     add_blocks(back_high, back_low, marks, grid)
-    grid_to_image(grid, tables, middle, maps, out)
-
-
-def normal_kernel(image, weight, kernel, column, tables, maps, out, marks, back_high, back_low, middle, grid, grid_high, grid_low):
+
+    def ready():
+        for copy in map_copies:
+            copy.wait_recv()
+
+    grid_to_image(grid, tables, middle, maps, out, ready)
+    for copy in sent:
+        copy.wait_send()
+
+
+def normal_kernel(image, info, kernel, tables, maps, out, marks, back_high, back_low, middle, grid, grid_high, grid_low):
     base = kernel.shape[0]
-    mark_blocks(column, marks)
+    mark_blocks(info, marks)
     image_to_grid(image, tables, middle, maps, grid_high, grid_low)
     kernel_high, kernel_low = split(kernel[...])
     turned_high, turned_low = split(kernel[...].T)
@@ -287,9 +363,12 @@
         start = pl.multiple_of(index * step, step)
         mark = marks[:, pl.ds(start, step)]
         picked = dot(grid_high[...], mark) + dot(grid_low[...], mark)
+        position = lax.broadcasted_iota(jnp.int32, (base, step), 0).astype(F32)
+        count, density = info[1:2, pl.ds(start, step)], info[2:3, pl.ds(start, step)]
+        weight = jnp.where(position < count, density, 0.0)
         for part in range(picked.shape[0] // base):
             rows = slice(part * base, (part + 1) * base)
-            value = dot_left(kernel_high, kernel_low, picked[rows]) * weight[:, pl.ds(start, step)]
+            value = dot_left(kernel_high, kernel_low, picked[rows]) * weight
             high, low = split(dot_left(turned_high, turned_low, value))
             back_high[rows, pl.ds(start, step)] = high
             back_low[rows, pl.ds(start, step)] = low
@@ -300,25 +379,49 @@
     grid_to_image(grid, tables, middle, maps, out)
 
 
-def call(kernel, map_shape, tiles, forward):
+def work_space(map_shape, tiles):
     coils, _, _, base, length = map_shape
     cells = RADIX * length
     rows = 2 * base * coils
-    scratch = [
+    return [
         pltpu.VMEM((cells, tiles), BF16),
         pltpu.VMEM((rows, tiles), BF16),
         pltpu.VMEM((rows, tiles), BF16),
         pltpu.VMEM((RADIX, 2 * base, coils * length), F32),
         pltpu.VMEM((rows, cells), F32),
+    ], pltpu.VMEM((rows, cells), BF16)
+
+
+def rhs_call(map_shape, tiles, slabs):
+    coils, _, _, base, length = map_shape
+    image = jax.ShapeDtypeStruct(map_shape[1:], F32)
+    whole = jax.ShapeDtypeStruct(map_shape, F32)
+    facts = jax.ShapeDtypeStruct((8, tiles), F32)
+    memory = pl.BlockSpec(memory_space=pltpu.VMEM)
+    scratch = [
+        pltpu.VMEM((2, 2 * coils, tiles, base), F32),
+        pltpu.VMEM((slabs, 8, tiles // slabs), F32),
     ]
-    if forward:
-        scratch += [pltpu.VMEM((rows, cells), BF16)] * 2
     return pl.pallas_call(
-        kernel,
+        rhs_kernel,
+        out_shape=(image, whole, facts),
+        in_specs=[memory] * 6,
+        out_specs=[memory] * 3,
+        scratch_shapes=scratch + work_space(map_shape, tiles)[0] + [pltpu.SemaphoreType.DMA((9,))] * 2,
+        compiler_params=pltpu.CompilerParams(
+            collective_id=2, has_side_effects=True, vmem_limit_bytes=56 * 2**20
+        ),
+    )
+
+
+def normal_call(map_shape, tiles):
+    scratch, half = work_space(map_shape, tiles)
+    return pl.pallas_call(
+        normal_kernel,
         out_shape=jax.ShapeDtypeStruct(map_shape[1:], F32),
-        in_specs=[pl.BlockSpec(memory_space=pltpu.VMEM)] * 6,
+        in_specs=[pl.BlockSpec(memory_space=pltpu.VMEM)] * 5,
         out_specs=pl.BlockSpec(memory_space=pltpu.VMEM),
-        scratch_shapes=scratch,
+        scratch_shapes=scratch + [half, half],
         compiler_params=pltpu.CompilerParams(vmem_limit_bytes=56 * 2**20),
     )
 
@@ -505,36 +608,30 @@
 
     near = coil_maps.reshape(pairs, group, 2, xpos, lines, RADIX, ylen).transpose(0, 3, 1, 2, 5, 4, 6)
     near = near.reshape(slabs, group, 2, RADIX, lines, ylen)
-    data = samples.reshape(pairs, 1, group * 2, *samples.shape[2:])
-    data = jnp.broadcast_to(data, (pairs, xpos, *data.shape[2:])).reshape(slabs, *data.shape[2:])
-    data = lax.all_to_all(data, "slab", split_axis=0, concat_axis=2, tiled=True)[0]
-    maps = lax.all_to_all(near, "slab", split_axis=0, concat_axis=4, tiled=True)[0]
-
-    cells = jnp.stack((tile_block, tile_count, dcf_level))
-    cells = lax.all_gather(cells, "slab", axis=1, tiled=True)
-    block, count, level = cells[0], cells[1], cells[2]
-    tiles = block.shape[0]
-    shard = jnp.arange(tiles, dtype=jnp.int32) // (tiles // slabs)
-    ky = shard * ky_dev + block // zblocks % ky_dev
-    column = block % zblocks * ylen + ky % RADIX * base + ky // RADIX
-    column = jnp.where(block // (zblocks * ky_dev) == slab % xpos, column, -1)[None, :]
+    data = samples.reshape(ncoil * 2, *samples.shape[2:])
+    shard_tiles = tile_block.shape[0]
+    tiles = shard_tiles * slabs
+    ky = slab * ky_dev + tile_block // zblocks % ky_dev
+    column = tile_block % zblocks * ylen + ky % RADIX * base + ky // RADIX
+    column = column + tile_block // (zblocks * ky_dev) * (zblocks * ylen)
     levels = jnp.arange(dcf_table.shape[0], dtype=jnp.int32)
-    density = jnp.sum(jnp.where(level[:, None] == levels[None, :], dcf_table[None, :], 0.0), axis=1)
+    density = jnp.sum(jnp.where(dcf_level[:, None] == levels[None, :], dcf_table[None, :], 0.0), axis=1)
     position = jnp.arange(base, dtype=jnp.int32)
-    weight = jnp.where(position[None, :] < count[:, None], density[:, None], 0.0)
-    weight_t = jnp.where(position[:, None] < count[None, :], density[None, :], 0.0)
+    weight = jnp.where(position[None, :] < tile_count[:, None], density[:, None], 0.0)
+    info = jnp.stack((column.astype(F32), tile_count.astype(F32), density))
+    info = jnp.concatenate((info, jnp.zeros((5, shard_tiles), F32)))
 
     tables = jnp.asarray(dft_tables(ylen))
-    shape = maps.shape
+    shape = (group, 2, RADIX, base, ylen)
     flat = (2 * RADIX * base, ylen)
 
-    partial = call(rhs_kernel, shape, tiles, False)(data, weight, kernel, column, tables, maps)
+    partial, maps, info = rhs_call(shape, tiles, slabs)(near, data, weight, info, kernel, tables)
     direction, norm = combine_call(True, flat)(partial.reshape(flat))
     residual, answer = direction, jnp.zeros_like(direction)
-    normal = call(normal_kernel, shape, tiles, True)
+    normal = normal_call(shape, tiles)
     update = combine_call(False, flat)
     for step in range(ITERS):
-        partial = normal(direction.reshape(shape[1:]), weight_t, kernel, column, tables, maps)
+        partial = normal(direction.reshape(shape[1:]), info, kernel, tables, maps)
         direction, residual, answer, norm = update(partial.reshape(flat), direction, residual, answer, norm)
 
     both = jnp.stack((answer, residual)).reshape(2, 2, RADIX, base, ylen)

time: 323 us -> 280 us (0.87)
  Pallas kernels: 174 us -> 250 us
  blocking collectives: 58.6 us -> 0 us
  waiting for transfers between devices: 56.8 us -> 13.9 us
  starting transfers between devices: 10 us -> 0.07 us
  local copies, waits for them, and re-layouts: 18.1 us -> 9.24 us
    pallas_call x3, Pallas kernels: 63.9 us -> 137 us  [the longest x1 86.4 us: whole_coils(): rhs_call(shape, tiles, slabs)(near, data, weight, info, kernel, tables)]
    all_gather x1 -> x0, blocking collectives: 58.6 us -> none  [whole_coils(): cells = lax.all_gather(cells, 'slab', axis=1, tiled=True)]
    all_to_all x2 -> x0, waiting for transfers between devices: 42.9 us -> none  [the longest x1 42.9 us: whole_coils(): lax.all_to_all(data, 'slab', split_axis=0, concat_axis=2, tiled=True)[0]]
    all_to_all x2 -> x0, starting transfers between devices: 9.95 us -> none  [the longest x1 6.32 us: whole_coils(): lax.all_to_all(data, 'slab', split_axis=0, concat_axis=2, tiled=True)[0]]
    all_to_all x2 -> x0, local copies, waits for them, and re-layouts: 4.74 us -> none  [the longest x1 3.1 us: whole_coils(): lax.all_to_all(data, 'slab', split_axis=0, concat_axis=2, tiled=True)[0]]
    pallas_call x1, Pallas kernels: 32.2 us -> 35.6 us  [whole_coils(): direction, norm = combine_call(True, flat)(partial.reshape(flat))]
    unnamed x17 -> x9, local copies, waits for them, and re-layouts: 6.58 us -> 5.22 us
  transfers between devices with their start and end apart: 3 -> 1, of which waited for: 2 -> 1; matrix products, arithmetic and copies ran while one was open for 3% -> 0% of each run, Pallas kernels for 0% -> 0%
where the time goes in v3:
time: 280 us; the launch traced here: 279 us
  Pallas kernels  250 us (89%)
  waiting for transfers between devices  13.9 us (5%)
  local copies, waits for them, and re-layouts  9.24 us (3%)
  other arithmetic  5.13 us (2%)
    pallas_call x1, Pallas kernels, whole_coils(): rhs_call(shape, tiles, slabs)(near, data, weight, info, kernel, tables)  86.4 us
    pallas_call x2, Pallas kernels, whole_coils(): update(partial.reshape(flat), direction, residual, answer, norm)  78 us
    pallas_call x2, Pallas kernels, whole_coils(): partial = normal(direction.reshape(shape[1:]), info, kernel, tables, maps)  50.3 us
    pallas_call x1, Pallas kernels, whole_coils(): direction, norm = combine_call(True, flat)(partial.reshape(flat))  35.6 us
    ppermute x1, waiting for transfers between devices, whole_coils(): lax.ppermute(give, 'slab', [(index, index ^ 1) for index in range(slabs)])  13.9 us
  transfers between devices with their start and end apart: 1, of which 1 were waited for; matrix products, arithmetic and copies ran while one was open for 0% of the time, Pallas kernels for 0%

profile of v3, /device:TPU:0, one launch (start us, length us, event | category | flops | bytes accessed | tf_op | source)
XLA Modules:
  0.0 279.3 jit_solution(4755905611114624913)
XLA Ops:
  0.6 0.7 convert_element_type.7
  1.3 0.8 select_reduce_fusion
  2.1 1.5 fusion.2.weight
  3.6 3.5 %copy.26 = f32[4,2,2,96,384]{4,2,3,1,0:T(2,128)S(1)} copy(f32[4,2,2,96,384]{4,3,2,1,0:T(8,128)} %param.8) | data formatting | bytes 4718592 | tf_op args[0]
  7.1 0.0 copy-start.2
  7.1 1.8 copy.27
  8.8 0.0 copy-done.2
  8.9 0.1 pad.7.clone
  9.0 0.7 maximum_maximum_fusion.own_info
  9.6 86.4 %shard_map.95 = (f32[2,3,128,384]{3,2,1,0:T(8,128)}, f32[2,2,3,128,384]{4,3,2,1,0:T(8,128)}, f32[8,1024]{1,0:T(8,128)}) custom-call(f32[4,2,2,3,32,384]{5,4,3,2,1,0:T(8,128)} %bitcast.24, f32[8,256,128]{2,1,0:T(8,128)} %bitcast.36, f32[256,128]{1,0:T(8,128)} %fusion.2.weight, f32[8,256]{1,0:T(8,128)} %maximum_maximum_fusion.own_info, f32[128,128]{1,0:T(8,128)} %kernel.5, ...), custom_call_target="tpu_custom_call" | custom-call | tf_op jit(solution)/shard_map/pallas_call | solution.py:628
  96.0 35.6 %shard_map.96 = (f32[768,384]{1,0:T(8,128)}, f32[8,128]{1,0:T(8,128)}) custom-call(f32[768,384]{1,0:T(8,128)} %bitcast.35), custom_call_target="tpu_custom_call" | custom-call | tf_op jit(solution)/shard_map/pallas_call | solution.py:629
  131.7 25.0 %shard_map.97 = f32[2,3,128,384]{3,2,1,0:T(8,128)} custom-call(f32[2,3,128,384]{3,2,1,0:T(8,128)} %bitcast.23, f32[8,1024]{1,0:T(8,128)} %get-tuple-element.15.info, f32[128,128]{1,0:T(8,128)} %kernel.5, bf16[3,4,2,256,256]{4,3,2,1,0:T(8,128)(2,1)} %constant.75.clone.tables, f32[2,2,3,128,384]{4,3,2,1,0:T(8,128)} %get-tuple-element.16.maps), custom_call_target="tpu_custom_call" | custom-call | tf_op jit(solution)/shard_map/pallas_call | solution.py:634
  156.7 1.2 broadcast_in_dim.41.refs_3_
  157.9 39.3 %shard_map.98 = (f32[768,384]{1,0:T(8,128)}, f32[768,384]{1,0:T(8,128)}, f32[768,384]{1,0:T(8,128)}, f32[8,128]{1,0:T(8,128)}) custom-call(f32[768,384]{1,0:T(8,128)} %bitcast.32, f32[768,384]{1,0:T(8,128)} %get-tuple-element.14.refs_1_.refs_2_, f32[768,384]{1,0:T(8,128)} %get-tuple-element.14.refs_1_.refs_2_, f32[768,384]{1,0:T(8,128)} %broadcast_in_dim.41.refs_3_, ...), custom_call_target="tpu_custom_call" | custom-call | tf_op jit(solution)/shard_map/pallas_call | solution.py:635
  197.1 25.3 %shard_map.99 = f32[2,3,128,384]{3,2,1,0:T(8,128)} custom-call(f32[2,3,128,384]{3,2,1,0:T(8,128)} %bitcast.30, f32[8,1024]{1,0:T(8,128)} %get-tuple-element.15.info, f32[128,128]{1,0:T(8,128)} %kernel.5, bf16[3,4,2,256,256]{4,3,2,1,0:T(8,128)(2,1)} %constant.75.clone.tables, f32[2,2,3,128,384]{4,3,2,1,0:T(8,128)} %get-tuple-element.16.maps), custom_call_target="tpu_custom_call" | custom-call | tf_op jit(solution)/shard_map/pallas_call | solution.py:634
  222.4 38.7 %shard_map.100 = (f32[768,384]{1,0:T(8,128)}, f32[768,384]{1,0:T(8,128)}, f32[768,384]{1,0:T(8,128)}, f32[8,128]{1,0:T(8,128)}) custom-call(f32[768,384]{1,0:T(8,128)} %bitcast.31, f32[768,384]{1,0:T(8,128)} %get-tuple-element.18.refs_1_, f32[768,384]{1,0:T(8,128)} %get-tuple-element.19.refs_2_, f32[768,384]{1,0:T(8,128)} %get-tuple-element.20.refs_3_, ...), custom_call_target="tpu_custom_call" | custom-call | tf_op jit(solution)/shard_map/pallas_call | solution.py:635
  261.1 0.0 copy-start
  261.1 0.0 copy-start.1
  261.1 1.3 fusion
  262.4 0.1 collective-permute-start
  262.5 13.9 %collective-permute-done = f32[2,2,3,32,384]{4,3,2,1,0:T(8,128)S(1)} collective-permute-done((f32[2,2,3,32,384]{4,3,2,1,0:T(8,128)S(1)}, f32[2,2,3,32,384]{4,3,2,1,0:T(8,128)S(1)}, u32[]{:S(2)}, u32[]{:S(2)}) %collective-permute-start) | collective-permute-done | bytes 589856 | tf_op jit(solution)/shard_map/ppermute | solution.py:641
  276.3 0.0 copy-done
  276.3 0.0 copy-done.1
  276.3 0.1 select_bitcast_fusion.1
  276.5 0.1 maximum_bitcast_fusion
  276.6 0.1 fusion.8
  276.7 0.5 copy.28
  277.2 0.9 copy.30
  278.0 0.5 copy.29
  278.5 0.9 copy.31
  (2 shorter events, 0.0 us)
Async XLA Ops:
  7.1 1.8 copy-start.2
  261.1 15.2 %copy-start = (f32[768,384]{1,0:T(8,128)S(1)}, f32[768,384]{1,0:T(8,128)}, u32[]{:S(2)}) copy-start(f32[768,384]{1,0:T(8,128)} %get-tuple-element.23) | copy-start | bytes 3538948
  261.1 15.2 %copy-start.1 = (f32[768,384]{1,0:T(8,128)S(1)}, f32[768,384]{1,0:T(8,128)}, u32[]{:S(2)}) copy-start(f32[768,384]{1,0:T(8,128)} %get-tuple-element.22) | copy-start | bytes 3538948
  262.4 14.0 %collective-permute-start = (f32[2,2,3,32,384]{4,3,2,1,0:T(8,128)S(1)}, f32[2,2,3,32,384]{4,3,2,1,0:T(8,128)S(1)}, u32[]{:S(2)}, u32[]{:S(2)}) collective-permute-start(f32[2,2,3,32,384]{4,3,2,1,0:T(8,128)S(1)} %fusion), channel_id=1, source_target_pairs={{0,4},{4,0},{8,12},{12,8},{1,5},{5,1},{9,13},{13,9},{2,6},{6,2},{1... | collective-permute-start | bytes 1769480 | tf_op jit(solution)/shard_map/ppermute | solution.py:641

commit v4 on v3

--- a/solution.py
+++ b/solution.py
@@ -270,7 +270,7 @@
                marks, back_high, back_low, middle, grid, send, recv):
     base = kernel.shape[0]
     shard_tiles = samples.shape[1]
-    lines = near_maps.shape[4]
+    lines = near_maps.shape[5]
     slab = lax.axis_index("slab")
     far, near = slab // 2, slab % 2
     others = ((1 - far) * 2 + near, far * 2 + (1 - near), (1 - far) * 2 + (1 - near))
@@ -312,8 +312,8 @@
     map_copies = []
     for index in (2, 0, 1):
         other = others[index]
-        map_copies.append(push(near_maps.at[other], maps.at[:, :, :, lines_of(slab), :], 6 + index, other))
-    maps[:, :, :, lines_of(slab), :] = near_maps[slab]
+        map_copies.append(push(near_maps.at[other // 2, :, :, other % 2], maps.at[:, :, :, lines_of(slab), :], 6 + index, other))
+    maps[:, :, :, lines_of(slab), :] = near_maps[far, :, :, near]
     arrived[slab] = own_info[...]
     for copy in info_copies:
         copy.wait_recv()
@@ -470,40 +470,38 @@
         sent.append(copy)
         return copy
 
-    orders = [(0, 1, 2) if chunk % 2 == 0 else (0, 2, 1) for chunk in range(CHUNKS)]
     starts = [chunk * size for chunk in range(CHUNKS)]
     flying = [None] * CHUNKS
     place = [0, size // 2, size // 2 + size // 4]
-    slots = [[None] * 3 for _ in range(CHUNKS)]
-    for stage in range(4):
+
+    def advance(chunk, stage):
+        if stage:
+            flying[chunk].wait_recv()
+        if 1 <= stage <= 3:
+            count = size >> stage
+            mine = rows(starts[chunk], count)
+            arrived = landed[chunk, place[stage - 1] : place[stage - 1] + count, :]
+            held = part if stage == 1 else work
+            goal = whole if stage == 3 else work
+            goal[mine, :] = held[mine, :] + arrived
+        if stage < 3:
+            half = size >> (stage + 1)
+            other = starts[chunk] + (1 - bits[stage]) * half
+            source = part if stage == 0 else work
+            target = landed.at[chunk, pl.ds(place[stage], half), :]
+            flying[chunk] = push(source.at[rows(other, half), :], target, chunk * 6 + stage, stage)
+            starts[chunk] = starts[chunk] + bits[stage] * half
+        else:
+            if stage > 3:
+                starts[chunk] = starts[chunk] - bits[6 - stage] * (size >> (7 - stage))
+            if stage < 6:
+                mine = whole.at[rows(starts[chunk], size >> (6 - stage)), :]
+                flying[chunk] = push(mine, mine, chunk * 6 + stage, 5 - stage)
+
+    for front in range(7 + CHUNKS - 1):
         for chunk in range(CHUNKS):
-            count = size >> stage
-            if stage:
-                flying[chunk].wait_recv()
-                mine = rows(starts[chunk], count)
-                arrived = landed[chunk, place[stage - 1] : place[stage - 1] + count, :]
-                held = part if stage == 1 else work
-                goal = whole if stage == 3 else work
-                goal[mine, :] = held[mine, :] + arrived
-            if stage < 3:
-                half = count // 2
-                bit = bits[orders[chunk][stage]]
-                other = starts[chunk] + (1 - bit) * half
-                source = part if stage == 0 else work
-                target = landed.at[chunk, pl.ds(place[stage], half), :]
-                flying[chunk] = push(source.at[rows(other, half), :], target, chunk * 6 + stage, orders[chunk][stage])
-                starts[chunk] = starts[chunk] + bit * half
-    for stage in range(4):
-        for chunk in range(CHUNKS):
-            if stage:
-                flying[chunk].wait_recv()
-                axis = orders[chunk][3 - stage]
-                starts[chunk] = starts[chunk] - bits[axis] * (size >> (4 - stage))
-            if stage < 3:
-                axis = orders[chunk][2 - stage]
-                mine = whole.at[rows(starts[chunk], size >> (3 - stage)), :]
-                flying[chunk] = push(mine, mine, chunk * 6 + 3 + stage, axis)
-
+            if 0 <= front - chunk < 7:
+                advance(chunk, front - chunk)
     for copy in sent:
         copy.wait_send()
     sent.clear()
@@ -606,8 +604,7 @@
     pairs = slabs // xpos
     group = ncoil // pairs
 
-    near = coil_maps.reshape(pairs, group, 2, xpos, lines, RADIX, ylen).transpose(0, 3, 1, 2, 5, 4, 6)
-    near = near.reshape(slabs, group, 2, RADIX, lines, ylen)
+    near = coil_maps.reshape(pairs, group, 2, xpos, lines, RADIX, ylen).transpose(0, 1, 2, 3, 5, 4, 6)
     data = samples.reshape(ncoil * 2, *samples.shape[2:])
     shard_tiles = tile_block.shape[0]
     tiles = shard_tiles * slabs

time: 280 us -> 289 us (1.032)
  Pallas kernels: 250 us -> 260 us
    pallas_call x2, Pallas kernels: 78 us -> 84.1 us  [whole_coils(): update(partial.reshape(flat), direction, residual, answer, norm)]
    pallas_call x1, Pallas kernels: 35.6 us -> 39.1 us  [whole_coils(): direction, norm = combine_call(True, flat)(partial.reshape(flat))]
where the time goes in v4:
time: 289 us
  Pallas kernels  260 us (90%)
  waiting for transfers between devices  13.8 us (5%)
  local copies, waits for them, and re-layouts  9.21 us (3%)
  other arithmetic  5.13 us (2%)
    pallas_call x1, Pallas kernels, whole_coils(): rhs_call(shape, tiles, slabs)(near, data, weight, info, kernel, tables)  86.4 us
    pallas_call x2, Pallas kernels, whole_coils(): update(partial.reshape(flat), direction, residual, answer, norm)  84.1 us
    pallas_call x2, Pallas kernels, whole_coils(): partial = normal(direction.reshape(shape[1:]), info, kernel, tables, maps)  50.3 us
    pallas_call x1, Pallas kernels, whole_coils(): direction, norm = combine_call(True, flat)(partial.reshape(flat))  39.1 us
    ppermute x1, waiting for transfers between devices, whole_coils(): lax.ppermute(give, 'slab', [(index, index ^ 1) for index in range(slabs)])  13.8 us
  transfers between devices with their start and end apart: 1, of which 1 were waited for; matrix products, arithmetic and copies ran while one was open for 0% of the time, Pallas kernels for 0%

profile of v4, /device:TPU:0, one launch (start us, length us, event | category | flops | bytes accessed | tf_op | source)
XLA Modules:
  0.0 288.9 jit_solution(17159586279579964167)
XLA Ops:
  0.6 0.7 convert_element_type.7
  1.3 0.8 select_reduce_fusion
  2.1 1.5 fusion.2.weight
  3.6 3.5 %copy.25 = f32[4,2,2,96,384]{4,2,3,1,0:T(2,128)S(1)} copy(f32[4,2,2,96,384]{4,3,2,1,0:T(8,128)} %param.8) | data formatting | bytes 4718592 | tf_op args[0]
  7.1 0.0 copy-start.2
  7.1 1.7 copy.32
  8.8 0.0 copy-done.2
  8.9 0.1 pad.7.clone
  8.9 0.7 maximum_maximum_fusion.own_info
  9.6 86.4 %shard_map.95 = (f32[2,3,128,384]{3,2,1,0:T(8,128)}, f32[2,2,3,128,384]{4,3,2,1,0:T(8,128)}, f32[8,1024]{1,0:T(8,128)}) custom-call(f32[2,2,2,2,3,32,384]{6,5,4,3,2,1,0:T(8,128)} %bitcast.24, f32[8,256,128]{2,1,0:T(8,128)} %bitcast.36, f32[256,128]{1,0:T(8,128)} %fusion.2.weight, f32[8,256]{1,0:T(8,128)} %maximum_maximum_fusion.own_info, f32[128,128]{1,0:T(8,128)} %kernel.5, ...), custom_call_target="tpu_custom_call" | custom-call | tf_op jit(solution)/shard_map/pallas_call | solution.py:625
  96.0 39.1 %shard_map.96 = (f32[768,384]{1,0:T(8,128)}, f32[8,128]{1,0:T(8,128)}) custom-call(f32[768,384]{1,0:T(8,128)} %bitcast.35), custom_call_target="tpu_custom_call" | custom-call | tf_op jit(solution)/shard_map/pallas_call | solution.py:626
  135.1 25.0 %shard_map.97 = f32[2,3,128,384]{3,2,1,0:T(8,128)} custom-call(f32[2,3,128,384]{3,2,1,0:T(8,128)} %bitcast.23, f32[8,1024]{1,0:T(8,128)} %get-tuple-element.15.info, f32[128,128]{1,0:T(8,128)} %kernel.5, bf16[3,4,2,256,256]{4,3,2,1,0:T(8,128)(2,1)} %constant.75.clone.tables, f32[2,2,3,128,384]{4,3,2,1,0:T(8,128)} %get-tuple-element.16.maps), custom_call_target="tpu_custom_call" | custom-call | tf_op jit(solution)/shard_map/pallas_call | solution.py:631
  160.2 1.2 broadcast_in_dim.41.refs_3_
  161.3 43.1 %shard_map.98 = (f32[768,384]{1,0:T(8,128)}, f32[768,384]{1,0:T(8,128)}, f32[768,384]{1,0:T(8,128)}, f32[8,128]{1,0:T(8,128)}) custom-call(f32[768,384]{1,0:T(8,128)} %bitcast.32, f32[768,384]{1,0:T(8,128)} %get-tuple-element.14.refs_1_.refs_2_, f32[768,384]{1,0:T(8,128)} %get-tuple-element.14.refs_1_.refs_2_, f32[768,384]{1,0:T(8,128)} %broadcast_in_dim.41.refs_3_, ...), custom_call_target="tpu_custom_call" | custom-call | tf_op jit(solution)/shard_map/pallas_call | solution.py:632
  204.4 25.3 %shard_map.99 = f32[2,3,128,384]{3,2,1,0:T(8,128)} custom-call(f32[2,3,128,384]{3,2,1,0:T(8,128)} %bitcast.30, f32[8,1024]{1,0:T(8,128)} %get-tuple-element.15.info, f32[128,128]{1,0:T(8,128)} %kernel.5, bf16[3,4,2,256,256]{4,3,2,1,0:T(8,128)(2,1)} %constant.75.clone.tables, f32[2,2,3,128,384]{4,3,2,1,0:T(8,128)} %get-tuple-element.16.maps), custom_call_target="tpu_custom_call" | custom-call | tf_op jit(solution)/shard_map/pallas_call | solution.py:631
  229.7 41.0 %shard_map.100 = (f32[768,384]{1,0:T(8,128)}, f32[768,384]{1,0:T(8,128)}, f32[768,384]{1,0:T(8,128)}, f32[8,128]{1,0:T(8,128)}) custom-call(f32[768,384]{1,0:T(8,128)} %bitcast.31, f32[768,384]{1,0:T(8,128)} %get-tuple-element.18.refs_1_, f32[768,384]{1,0:T(8,128)} %get-tuple-element.19.refs_2_, f32[768,384]{1,0:T(8,128)} %get-tuple-element.20.refs_3_, ...), custom_call_target="tpu_custom_call" | custom-call | tf_op jit(solution)/shard_map/pallas_call | solution.py:632
  270.7 0.0 copy-start
  270.7 0.0 copy-start.1
  270.7 1.3 fusion
  272.0 0.2 collective-permute-start
  272.1 13.8 %collective-permute-done = f32[2,2,3,32,384]{4,3,2,1,0:T(8,128)S(1)} collective-permute-done((f32[2,2,3,32,384]{4,3,2,1,0:T(8,128)S(1)}, f32[2,2,3,32,384]{4,3,2,1,0:T(8,128)S(1)}, u32[]{:S(2)}, u32[]{:S(2)}) %collective-permute-start) | collective-permute-done | bytes 589856 | tf_op jit(solution)/shard_map/ppermute | solution.py:638
  285.9 0.0 copy-done
  285.9 0.0 copy-done.1
  285.9 0.1 select_bitcast_fusion.1
  286.1 0.1 maximum_bitcast_fusion
  286.2 0.1 fusion.8
  286.3 0.5 copy.27
  286.8 0.9 copy.29
  287.6 0.5 copy.28
  288.1 0.9 copy.30
  (2 shorter events, 0.0 us)
Async XLA Ops:
  7.1 1.7 copy-start.2
  270.7 15.2 %copy-start = (f32[768,384]{1,0:T(8,128)S(1)}, f32[768,384]{1,0:T(8,128)}, u32[]{:S(2)}) copy-start(f32[768,384]{1,0:T(8,128)} %get-tuple-element.23) | copy-start | bytes 3538948
  270.7 15.2 %copy-start.1 = (f32[768,384]{1,0:T(8,128)S(1)}, f32[768,384]{1,0:T(8,128)}, u32[]{:S(2)}) copy-start(f32[768,384]{1,0:T(8,128)} %get-tuple-element.22) | copy-start | bytes 3538948
  272.0 14.0 %collective-permute-start = (f32[2,2,3,32,384]{4,3,2,1,0:T(8,128)S(1)}, f32[2,2,3,32,384]{4,3,2,1,0:T(8,128)S(1)}, u32[]{:S(2)}, u32[]{:S(2)}) collective-permute-start(f32[2,2,3,32,384]{4,3,2,1,0:T(8,128)S(1)} %fusion), channel_id=1, source_target_pairs={{0,4},{4,0},{8,12},{12,8},{1,5},{5,1},{9,13},{13,9},{2,6},{6,2},{1... | collective-permute-start | bytes 1769480 | tf_op jit(solution)/shard_map/ppermute | solution.py:638

commit v5 on v3

--- a/solution.py
+++ b/solution.py
@@ -195,6 +195,10 @@
     lax.fori_loop(0, marks.shape[0] // step, chunk, 0)
 
 
+def image_rows(part, b, base):
+    return pl.ds(pl.multiple_of((part * RADIX + b) * base, base), base)
+
+
 def grid_to_image(grid, tables, middle, maps, out, ready=None):
     coils, _, _, base, length = maps.shape
     for c in range(coils):
@@ -228,7 +232,7 @@
                 sums[q] = term
         for q in range(RADIX):
             lanes = slice(q * base, (q + 1) * base)
-            out[0, b, :, lanes], out[1, b, :, lanes] = sums[q]
+            out[image_rows(0, b, base), lanes], out[image_rows(1, b, base), lanes] = sums[q]
         return carry
 
     lax.fori_loop(0, RADIX, rows, 0)
@@ -243,7 +247,7 @@
             for q in range(RADIX):
                 lanes = slice(q * base, (q + 1) * base)
                 map_r, map_i = maps[c, 0, b, :, lanes], maps[c, 1, b, :, lanes]
-                re, im = image[0, b, :, lanes], image[1, b, :, lanes]
+                re, im = image[image_rows(0, b, base), lanes], image[image_rows(1, b, base), lanes]
                 parts.append((map_r * re - map_i * im, map_r * im + map_i * re))
             for r, (re, im) in enumerate(butterfly(parts, -1.0)):
                 value = dot_right(jnp.concatenate((re, im), 1), tables[r, 2, 0], tables[r, 2, 1])
@@ -266,19 +270,14 @@
             grid_low[rows_c, lanes] = low
 
 
-def rhs_kernel(near_maps, samples, weight, own_info, kernel, tables, out, maps, info, data, arrived,
+def adjoint_of_samples(near_maps, samples, weight, own_info, kernel, tables, out, maps, info, data, arrived,
                marks, back_high, back_low, middle, grid, send, recv):
     base = kernel.shape[0]
     shard_tiles = samples.shape[1]
-    lines = near_maps.shape[4]
+    lines = near_maps.shape[5]
     slab = lax.axis_index("slab")
     far, near = slab // 2, slab % 2
     others = ((1 - far) * 2 + near, far * 2 + (1 - near), (1 - far) * 2 + (1 - near))
-    barrier = pltpu.get_barrier_semaphore()
-    for other in others:
-        pl.semaphore_signal(barrier, inc=1, device_id={"slab": other}, device_id_type=pl.DeviceIdType.MESH)
-    pl.semaphore_wait(barrier, len(others))
-
     sent = []
 
     def push(source, target, slot, other):
@@ -312,8 +311,8 @@
     map_copies = []
     for index in (2, 0, 1):
         other = others[index]
-        map_copies.append(push(near_maps.at[other], maps.at[:, :, :, lines_of(slab), :], 6 + index, other))
-    maps[:, :, :, lines_of(slab), :] = near_maps[slab]
+        map_copies.append(push(near_maps.at[other // 2, :, :, other % 2], maps.at[:, :, :, lines_of(slab), :], 6 + index, other))
+    maps[:, :, :, lines_of(slab), :] = near_maps[far, :, :, near]
     arrived[slab] = own_info[...]
     for copy in info_copies:
         copy.wait_recv()
@@ -351,9 +350,8 @@
         copy.wait_send()
 
 
-def normal_kernel(image, info, kernel, tables, maps, out, marks, back_high, back_low, middle, grid, grid_high, grid_low):
+def normal(image, info, kernel, tables, maps, out, marks, back_high, back_low, middle, grid, grid_high, grid_low):
     base = kernel.shape[0]
-    mark_blocks(info, marks)
     image_to_grid(image, tables, middle, maps, grid_high, grid_low)
     kernel_high, kernel_low = split(kernel[...])
     turned_high, turned_low = split(kernel[...].T)
@@ -379,63 +377,13 @@
     grid_to_image(grid, tables, middle, maps, out)
 
 
-def work_space(map_shape, tiles):
-    coils, _, _, base, length = map_shape
-    cells = RADIX * length
-    rows = 2 * base * coils
-    return [
-        pltpu.VMEM((cells, tiles), BF16),
-        pltpu.VMEM((rows, tiles), BF16),
-        pltpu.VMEM((rows, tiles), BF16),
-        pltpu.VMEM((RADIX, 2 * base, coils * length), F32),
-        pltpu.VMEM((rows, cells), F32),
-    ], pltpu.VMEM((rows, cells), BF16)
-
-
-def rhs_call(map_shape, tiles, slabs):
-    coils, _, _, base, length = map_shape
-    image = jax.ShapeDtypeStruct(map_shape[1:], F32)
-    whole = jax.ShapeDtypeStruct(map_shape, F32)
-    facts = jax.ShapeDtypeStruct((8, tiles), F32)
-    memory = pl.BlockSpec(memory_space=pltpu.VMEM)
-    scratch = [
-        pltpu.VMEM((2, 2 * coils, tiles, base), F32),
-        pltpu.VMEM((slabs, 8, tiles // slabs), F32),
-    ]
-    return pl.pallas_call(
-        rhs_kernel,
-        out_shape=(image, whole, facts),
-        in_specs=[memory] * 6,
-        out_specs=[memory] * 3,
-        scratch_shapes=scratch + work_space(map_shape, tiles)[0] + [pltpu.SemaphoreType.DMA((9,))] * 2,
-        compiler_params=pltpu.CompilerParams(
-            collective_id=2, has_side_effects=True, vmem_limit_bytes=56 * 2**20
-        ),
-    )
-
-
-def normal_call(map_shape, tiles):
-    scratch, half = work_space(map_shape, tiles)
-    return pl.pallas_call(
-        normal_kernel,
-        out_shape=jax.ShapeDtypeStruct(map_shape[1:], F32),
-        in_specs=[pl.BlockSpec(memory_space=pltpu.VMEM)] * 5,
-        out_specs=pl.BlockSpec(memory_space=pltpu.VMEM),
-        scratch_shapes=scratch + [half, half],
-        compiler_params=pltpu.CompilerParams(vmem_limit_bytes=56 * 2**20),
-    )
-
-
 CHUNKS = 4
 STEP = 96
 
 
-def combine(first, refs):
-    if first:
-        part, direction_out, norm_out, whole, landed, work, tile, send, recv = refs
-    else:
-        (part, direction, residual, answer, norm, direction_out, residual_out, answer_out, norm_out,
-         whole, landed, work, tile, send, recv) = refs
+def combine(turn_index, part, direction, residual, answer, norm, whole, landed, work, tile, send, recv):
+    first = turn_index == 0
+    base_slot = turn_index * (CHUNKS * 6 + 2)
     slab, coil = lax.axis_index("slab"), lax.axis_index("coil")
     core, chip, far, near = coil % 2, coil // 2, slab // 2, slab % 2
     partners = (
@@ -445,11 +393,6 @@
         {"slab": far * 2 + (1 - near)},
     )
     bits = (core, chip, far)
-    barrier = pltpu.get_barrier_semaphore()
-    for partner in partners:
-        pl.semaphore_signal(barrier, inc=1, device_id=partner, device_id_type=pl.DeviceIdType.MESH)
-    pl.semaphore_wait(barrier, len(partners))
-
     total = part.shape[0]
     size = total // CHUNKS
     sent = []
@@ -461,8 +404,8 @@
         copy = pltpu.make_async_remote_copy(
             src_ref=source,
             dst_ref=target,
-            send_sem=send.at[slot],
-            recv_sem=recv.at[slot],
+            send_sem=send.at[base_slot + slot],
+            recv_sem=recv.at[base_slot + slot],
             device_id=partners[axis],
             device_id_type=pl.DeviceIdType.MESH,
         )
@@ -509,10 +452,11 @@
     sent.clear()
 
     def exchange(value, index):
-        tile[index, 0] = jnp.broadcast_to(value, tile.shape[2:])
-        copy = push(tile.at[index, 0], tile.at[index, 1], CHUNKS * 6 + index, 3)
+        slot = turn_index * 2 + index
+        tile[slot, 0] = jnp.broadcast_to(value, tile.shape[2:])
+        copy = push(tile.at[slot, 0], tile.at[slot, 1], CHUNKS * 6 + index, 3)
         copy.wait_recv()
-        return (tile[index, 0] + tile[index, 1])[:1, :1]
+        return (tile[slot, 0] + tile[slot, 1])[:1, :1]
 
     def sweep(body):
         def step(index, carry):
@@ -528,10 +472,12 @@
 
         def copy_out(at):
             value = whole[at, :]
-            direction_out[at, :] = value
+            direction[at, :] = value
+            residual[at, :] = value
+            answer[at, :] = jnp.zeros_like(value)
             return fold(value * value)
 
-        norm_out[...] = jnp.broadcast_to(exchange(sweep(copy_out), 0), norm_out.shape)
+        norm[...] = jnp.broadcast_to(exchange(sweep(copy_out), 0), norm.shape)
     else:
 
         def meet(at):
@@ -545,8 +491,8 @@
 
         def shrink(at):
             left = residual[at, :] - alpha * work[at, :]
-            residual_out[at, :] = left
-            answer_out[at, :] = answer[at, :] + alpha * direction[at, :]
+            residual[at, :] = left
+            answer[at, :] = answer[at, :] + alpha * direction[at, :]
             return fold(left * left)
 
         after = exchange(sweep(shrink), 1)
@@ -554,43 +500,80 @@
 
         def turn(index, carry):
             at = rows(index * STEP, STEP)
-            direction_out[at, :] = residual_out[at, :] + beta * direction[at, :]
+            direction[at, :] = residual[at, :] + beta * direction[at, :]
             return carry
 
         lax.fori_loop(0, total // STEP, turn, 0)
-        norm_out[...] = jnp.broadcast_to(after, norm_out.shape)
+        norm[...] = jnp.broadcast_to(after, norm.shape)
     for copy in sent:
         copy.wait_send()
 
 
-def first_kernel(*refs):
-    combine(True, refs)
-
-
-def next_kernel(*refs):
-    combine(False, refs)
-
-
-def combine_call(first, shape):
-    image = jax.ShapeDtypeStruct(shape, F32)
-    scalar = jax.ShapeDtypeStruct((8, 128), F32)
-    copies = CHUNKS * 6 + 2
+def whole_kernel(near_maps, samples, weight, own_info, kernel, tables, answer, residual, maps, info, data, arrived,
+                 marks, back_high, back_low, middle, grid, grid_high, grid_low, part, direction, norm, whole, landed,
+                 work, tile, map_send, map_recv, send, recv):
+    slab, coil = lax.axis_index("slab"), lax.axis_index("coil")
+    core, chip, far, near = coil % 2, coil // 2, slab // 2, slab % 2
+    partners = (
+        {"coil": chip * 2 + (1 - core)},
+        {"coil": (1 - chip) * 2 + core},
+        {"slab": (1 - far) * 2 + near},
+        {"slab": far * 2 + (1 - near)},
+        {"slab": (1 - far) * 2 + (1 - near)},
+    )
+    barrier = pltpu.get_barrier_semaphore()
+    for partner in partners:
+        pl.semaphore_signal(barrier, inc=1, device_id=partner, device_id_type=pl.DeviceIdType.MESH)
+    pl.semaphore_wait(barrier, len(partners))
+    space = (marks, back_high, back_low, middle, grid)
+    sums = (part, direction, residual, answer, norm, whole, landed, work, tile, send, recv)
+    adjoint_of_samples(near_maps, samples, weight, own_info, kernel, tables, part, maps, info, data, arrived,
+                       *space, map_send, map_recv)
+    combine(0, *sums)
+    for step in range(ITERS):
+        normal(direction, info, kernel, tables, maps, part, *space, grid_high, grid_low)
+        combine(step + 1, *sums)
+
+
+def whole_call(map_shape, tiles, slabs):
+    coils, _, _, base, length = map_shape
+    cells = RADIX * length
+    rows = 2 * base * coils
+    flat = (2 * RADIX * base, length)
+    copies = (ITERS + 1) * (CHUNKS * 6 + 2)
+    image = pltpu.VMEM(flat, F32)
     memory = pl.BlockSpec(memory_space=pltpu.VMEM)
     return pl.pallas_call(
-        first_kernel if first else next_kernel,
-        out_shape=(image, scalar) if first else (image, image, image, scalar),
-        in_specs=[memory] * (1 if first else 5),
-        out_specs=[memory] * (2 if first else 4),
+        whole_kernel,
+        out_shape=(jax.ShapeDtypeStruct(flat, F32), jax.ShapeDtypeStruct(flat, F32)),
+        in_specs=[memory] * 6,
+        out_specs=[memory] * 2,
         scratch_shapes=[
-            pltpu.VMEM(shape, F32),
-            pltpu.VMEM((CHUNKS, shape[0] // CHUNKS, shape[1]), F32),
-            pltpu.VMEM(shape, F32),
-            pltpu.VMEM((2, 2, 8, 128), F32),
+            pltpu.VMEM(map_shape, F32),
+            pltpu.VMEM((8, tiles), F32),
+            pltpu.VMEM((2, 2 * coils, tiles, base), F32),
+            pltpu.VMEM((slabs, 8, tiles // slabs), F32),
+            pltpu.VMEM((cells, tiles), BF16),
+            pltpu.VMEM((rows, tiles), BF16),
+            pltpu.VMEM((rows, tiles), BF16),
+            pltpu.VMEM((RADIX, 2 * base, coils * length), F32),
+            pltpu.VMEM((rows, cells), F32),
+            pltpu.VMEM((rows, cells), BF16),
+            pltpu.VMEM((rows, cells), BF16),
+            image,
+            image,
+            pltpu.VMEM((8, 128), F32),
+            image,
+            pltpu.VMEM((CHUNKS, flat[0] // CHUNKS, length), F32),
+            image,
+            pltpu.VMEM((2 * ITERS + 2, 2, 8, 128), F32),
+            pltpu.SemaphoreType.DMA((9,)),
+            pltpu.SemaphoreType.DMA((9,)),
             pltpu.SemaphoreType.DMA((copies,)),
             pltpu.SemaphoreType.DMA((copies,)),
         ],
         compiler_params=pltpu.CompilerParams(
-            collective_id=0 if first else 1, has_side_effects=True, vmem_limit_bytes=56 * 2**20
+            collective_id=0, has_side_effects=True, vmem_limit_bytes=60 * 2**20
         ),
     )
 
@@ -606,8 +589,7 @@
     pairs = slabs // xpos
     group = ncoil // pairs
 
-    near = coil_maps.reshape(pairs, group, 2, xpos, lines, RADIX, ylen).transpose(0, 3, 1, 2, 5, 4, 6)
-    near = near.reshape(slabs, group, 2, RADIX, lines, ylen)
+    near = coil_maps.reshape(pairs, group, 2, xpos, lines, RADIX, ylen).transpose(0, 1, 2, 3, 5, 4, 6)
     data = samples.reshape(ncoil * 2, *samples.shape[2:])
     shard_tiles = tile_block.shape[0]
     tiles = shard_tiles * slabs
@@ -623,16 +605,7 @@
 
     tables = jnp.asarray(dft_tables(ylen))
     shape = (group, 2, RADIX, base, ylen)
-    flat = (2 * RADIX * base, ylen)
-
-    partial, maps, info = rhs_call(shape, tiles, slabs)(near, data, weight, info, kernel, tables)
-    direction, norm = combine_call(True, flat)(partial.reshape(flat))
-    residual, answer = direction, jnp.zeros_like(direction)
-    normal = normal_call(shape, tiles)
-    update = combine_call(False, flat)
-    for step in range(ITERS):
-        partial = normal(direction.reshape(shape[1:]), info, kernel, tables, maps)
-        direction, residual, answer, norm = update(partial.reshape(flat), direction, residual, answer, norm)
+    answer, residual = whole_call(shape, tiles, slabs)(near, data, weight, info, kernel, tables)
 
     both = jnp.stack((answer, residual)).reshape(2, 2, RADIX, base, ylen)
     partner = slab + 1 - 2 * (slab % 2)

time: 280 us -> 248 us (0.89)
  Pallas kernels: 250 us -> 220 us
    pallas_call x6 -> x1, Pallas kernels: 250 us -> 220 us  [whole_coils(): whole_call(shape, tiles, slabs)(near, data, weight, info, kernel, tables)]
where the time goes in v5:
time: 248 us
  Pallas kernels  220 us (89%)
  waiting for transfers between devices  13.9 us (6%)
  local copies, waits for them, and re-layouts  8.05 us (3%)
  other arithmetic  5.13 us (2%)
    pallas_call x1, Pallas kernels, whole_coils(): whole_call(shape, tiles, slabs)(near, data, weight, info, kernel, tables)  220 us
    ppermute x1, waiting for transfers between devices, whole_coils(): lax.ppermute(give, 'slab', [(index, index ^ 1) for index in range(slabs)])  13.9 us
    unnamed x9, local copies, waits for them, and re-layouts  5.22 us
  transfers between devices with their start and end apart: 1, of which 1 were waited for; matrix products, arithmetic and copies ran while one was open for 0% of the time, Pallas kernels for 0%

profile of v5, /device:TPU:0, one launch (start us, length us, event | category | flops | bytes accessed | tf_op | source)
XLA Modules:
  0.0 248.2 jit_solution(2560937315882132773)
XLA Ops:
  0.6 0.7 convert_element_type.7
  1.3 0.8 select_reduce_fusion
  2.1 1.5 fusion.2.weight
  3.6 3.5 %copy.25 = f32[4,2,2,96,384]{4,2,3,1,0:T(2,128)S(1)} copy(f32[4,2,2,96,384]{4,3,2,1,0:T(8,128)} %param.8) | data formatting | bytes 4718592 | tf_op args[0]
  7.1 0.0 copy-start.2
  7.1 1.7 copy.32
  8.8 0.0 copy-done.2
  8.9 0.1 pad.7.clone
  9.0 0.7 maximum_maximum_fusion.own_info
  9.6 220.4 %shard_map.95 = (f32[768,384]{1,0:T(8,128)}, f32[768,384]{1,0:T(8,128)}) custom-call(f32[2,2,2,2,3,32,384]{6,5,4,3,2,1,0:T(8,128)} %bitcast.18, f32[8,256,128]{2,1,0:T(8,128)} %bitcast.26, f32[256,128]{1,0:T(8,128)} %fusion.2.weight, f32[8,256]{1,0:T(8,128)} %maximum_maximum_fusion.own_info, f32[128,128]{1,0:T(8,128)} %kernel.1, ...), custom_call_target="tpu_custom_call" | custom-call | tf_op jit(solution)/shard_map/pallas_call | solution.py:608
  230.0 0.0 copy-start
  230.0 0.0 copy-start.1
  230.0 1.3 fusion
  231.3 0.1 collective-permute-start
  231.4 13.9 %collective-permute-done = f32[2,2,3,32,384]{4,3,2,1,0:T(8,128)S(1)} collective-permute-done((f32[2,2,3,32,384]{4,3,2,1,0:T(8,128)S(1)}, f32[2,2,3,32,384]{4,3,2,1,0:T(8,128)S(1)}, u32[]{:S(2)}, u32[]{:S(2)}) %collective-permute-start) | collective-permute-done | bytes 589856 | tf_op jit(solution)/shard_map/ppermute | solution.py:614
  245.2 0.0 copy-done
  245.2 0.0 copy-done.1
  245.2 0.1 select_bitcast_fusion.1
  245.4 0.1 maximum_bitcast_fusion
  245.5 0.1 fusion.8
  245.6 0.5 copy.28
  246.1 0.9 copy.30
  246.9 0.5 copy.27
  247.4 0.9 copy.29
  (2 shorter events, 0.0 us)
Async XLA Ops:
  7.1 1.8 copy-start.2
  230.0 15.2 %copy-start = (f32[768,384]{1,0:T(8,128)S(1)}, f32[768,384]{1,0:T(8,128)}, u32[]{:S(2)}) copy-start(f32[768,384]{1,0:T(8,128)} %get-tuple-element.4) | copy-start | bytes 3538948
  230.0 15.2 %copy-start.1 = (f32[768,384]{1,0:T(8,128)S(1)}, f32[768,384]{1,0:T(8,128)}, u32[]{:S(2)}) copy-start(f32[768,384]{1,0:T(8,128)} %get-tuple-element.5) | copy-start | bytes 3538948
  231.3 14.0 %collective-permute-start = (f32[2,2,3,32,384]{4,3,2,1,0:T(8,128)S(1)}, f32[2,2,3,32,384]{4,3,2,1,0:T(8,128)S(1)}, u32[]{:S(2)}, u32[]{:S(2)}) collective-permute-start(f32[2,2,3,32,384]{4,3,2,1,0:T(8,128)S(1)} %fusion), channel_id=1, source_target_pairs={{0,4},{4,0},{8,12},{12,8},{1,5},{5,1},{9,13},{13,9},{2,6},{6,2},{1... | collective-permute-start | bytes 1769480 | tf_op jit(solution)/shard_map/ppermute | solution.py:614

commit v6 on v5

--- a/solution.py
+++ b/solution.py
@@ -611,7 +611,12 @@
     partner = slab + 1 - 2 * (slab % 2)
     keep = lax.dynamic_slice_in_dim(both, slab * lines, lines, 3)
     give = lax.dynamic_slice_in_dim(both, partner * lines, lines, 3)
-    take = lax.ppermute(give, "slab", [(index, index ^ 1) for index in range(slabs)])
+    core = lax.axis_index("coil") % 2
+    swap = [(index, index ^ 1) for index in range(lax.axis_size("coil"))]
+    half = lax.dynamic_index_in_dim(give, core, keepdims=False)
+    half = lax.ppermute(half, "slab", [(index, index ^ 1) for index in range(slabs)])
+    rest = lax.ppermute(half, "coil", swap)
+    take = jnp.stack((jnp.where(core == 0, half, rest), jnp.where(core == 0, rest, half)))
     low = slab % 2 == 0
     both = jnp.stack((jnp.where(low, keep, take), jnp.where(low, take, keep)), 2)
     both = both.transpose(0, 1, 2, 4, 3, 5).reshape(2, 2, xpos, zdev, ylen)

time: 248 us -> 244 us (0.984)
  waiting for transfers between devices: 13.9 us -> 9.14 us
    ppermute x1 -> x2, waiting for transfers between devices: 13.9 us -> 9.14 us  [the longest x1 7.56 us: whole_coils(): lax.ppermute(half, 'slab', [(index, index ^ 1) for index in range(slabs)])]
  transfers between devices with their start and end apart: 1 -> 2, of which waited for: 1 -> 2; matrix products, arithmetic and copies ran while one was open for 0% -> 0% of each run, Pallas kernels for 0% -> 0%
where the time goes in v6:
time: 244 us
  Pallas kernels  220 us (90%)
  waiting for transfers between devices  9.14 us (4%)
  local copies, waits for them, and re-layouts  8.04 us (3%)
  other arithmetic  5.11 us (2%)
    pallas_call x1, Pallas kernels, whole_coils(): whole_call(shape, tiles, slabs)(near, data, weight, info, kernel, tables)  220 us
    ppermute x1, waiting for transfers between devices, whole_coils(): lax.ppermute(half, 'slab', [(index, index ^ 1) for index in range(slabs)])  7.56 us
    unnamed x9, local copies, waits for them, and re-layouts  5.22 us
  transfers between devices with their start and end apart: 2, of which 2 were waited for; matrix products, arithmetic and copies ran while one was open for 0% of the time, Pallas kernels for 0%

profile of v6, /device:TPU:0, one launch (start us, length us, event | category | flops | bytes accessed | tf_op | source)
XLA Modules:
  0.0 243.5 jit_solution(5009531013999598356)
XLA Ops:
  0.7 0.7 convert_element_type.7
  1.3 0.8 select_reduce_fusion
  2.1 1.5 fusion.3.weight
  3.6 3.5 %copy.25 = f32[4,2,2,96,384]{4,2,3,1,0:T(2,128)S(1)} copy(f32[4,2,2,96,384]{4,3,2,1,0:T(8,128)} %param.8) | data formatting | bytes 4718592 | tf_op args[0]
  7.1 0.0 copy-start.2
  7.1 1.7 copy.32
  8.8 0.0 copy-done.2
  8.9 0.1 pad.9.clone
  9.0 0.7 maximum_maximum_fusion.own_info
  9.6 220.4 %shard_map.95 = (f32[768,384]{1,0:T(8,128)}, f32[768,384]{1,0:T(8,128)}) custom-call(f32[2,2,2,2,3,32,384]{6,5,4,3,2,1,0:T(8,128)} %bitcast.24, f32[8,256,128]{2,1,0:T(8,128)} %bitcast.32, f32[256,128]{1,0:T(8,128)} %fusion.3.weight, f32[8,256]{1,0:T(8,128)} %maximum_maximum_fusion.own_info, f32[128,128]{1,0:T(8,128)} %kernel.1, ...), custom_call_target="tpu_custom_call" | custom-call | tf_op jit(solution)/shard_map/pallas_call | solution.py:608
  230.0 0.0 copy-start.1
  230.0 1.2 fusion.2
  231.2 0.0 copy-start
  231.2 0.1 collective-permute-start
  231.3 7.6 %collective-permute-done = f32[2,3,32,384]{3,2,1,0:T(8,128)S(1)} collective-permute-done((f32[2,3,32,384]{3,2,1,0:T(8,128)S(1)}, f32[2,3,32,384]{3,2,1,0:T(8,128)S(1)}, u32[]{:S(2)}, u32[]{:S(2)}) %collective-permute-start) | collective-permute-done | bytes 294944 | tf_op jit(solution)/shard_map/ppermute | solution.py:617
  238.9 0.0 collective-permute-start.1
  238.9 1.6 collective-permute-done.1
  240.5 0.1 select_bitcast_fusion.3
  240.5 0.0 copy-done.1
  240.5 0.0 copy-done
  240.5 0.1 select_bitcast_fusion.1
  240.7 0.1 maximum_bitcast_fusion
  240.8 0.1 fusion.9
  240.9 0.5 copy.28
  241.4 0.9 copy.30
  242.2 0.5 copy.27
  242.7 0.9 copy.29
  (2 shorter events, 0.0 us)
Async XLA Ops:
  7.1 1.7 copy-start.2
  230.0 10.5 %copy-start.1 = (f32[768,384]{1,0:T(8,128)S(1)}, f32[768,384]{1,0:T(8,128)}, u32[]{:S(2)}) copy-start(f32[768,384]{1,0:T(8,128)} %get-tuple-element.5) | copy-start | bytes 3538948
  231.2 9.3 %copy-start = (f32[768,384]{1,0:T(8,128)S(1)}, f32[768,384]{1,0:T(8,128)}, u32[]{:S(2)}) copy-start(f32[768,384]{1,0:T(8,128)} %get-tuple-element.4) | copy-start | bytes 3538948
  231.2 7.6 %collective-permute-start = (f32[2,3,32,384]{3,2,1,0:T(8,128)S(1)}, f32[2,3,32,384]{3,2,1,0:T(8,128)S(1)}, u32[]{:S(2)}, u32[]{:S(2)}) collective-permute-start(f32[2,3,32,384]{3,2,1,0:T(8,128)S(1)} %fusion.2), channel_id=1, source_target_pairs={{0,4},{4,0},{8,12},{12,8},{1,5},{5,1},{9,13},{13,9},{2,6},{6,2},{1... | collective-permute-start | bytes 884744 | tf_op jit(solution)/shard_map/ppermute | solution.py:617
  238.9 1.6 collective-permute-start.1
